TPU v7x, 32 devices: a whole 2x2x4 slice. The times are simulated.
32 devices in a mesh: dp: 8 (over y, x, core), fsdp: 4 (over z).
Axes of the slice: x: 2, y: 2, z: 4, core: 2. Of those that a mesh axis runs over, the one named last changes fastest.
Arguments:
- query_pooled_states: bfloat16 [4, 128, 4096], P('fsdp', 'dp')
- passage_pooled_states: bfloat16 [4, 1024, 4096], P('fsdp', 'dp')
- query_attention_output: bfloat16 [4, 128, 4096], P('fsdp', 'dp'), may hold values from -0.059814453 to 0.059814453
- passage_attention_output: bfloat16 [4, 1024, 4096], P('fsdp', 'dp'), may hold values from -0.059814453 to 0.059814453
- positive_passage_row: int32 [4, 128], P('fsdp', 'dp'), may hold values from 0 to 127
- hard_negative_ids: int32 [4, 128, 64], P('fsdp', 'dp'), may hold values from 0 to 1023, as said below
- passage_home_row: int32 [4, 1024], P('fsdp'), may hold values from 0 to 1023, as said below
- adapter_down_weight: bfloat16 [16, 4096], P(None, 'fsdp'), may hold values from -0.09375 to 0.09375
- adapter_up_weight: bfloat16 [16, 4096], P(None, 'fsdp'), may hold values from -0.09375 to 0.09375
Outputs:
- grad_query_states: bfloat16 [4, 128, 4096], P('fsdp', 'dp')
- grad_passage_states: bfloat16 [4, 1024, 4096], P('fsdp', 'dp')
- adapter_down_gradient: float32 [16, 4096], P(None, 'fsdp')
- adapter_up_gradient: float32 [16, 4096], P(None, 'fsdp')
Inputs may be any that keep to these rules, and one draw needn't show every extreme that they name: In each group the row is a permutation: passage p is row passage_home_row[g, p] of passage_pooled_states[g]. `hard_negative_ids`: ids of passages of the same group. The queries of one index of dp name at most 8 distinct passages held by any one index of dp, and in every group one index of dp holds exactly 8 distinct passages named by the queries of each index of dp. A query's list may repeat an id. `positive_passage_row`: the positive of query q is held by the query's own index of dp.
All inputs are finite; a program needn't handle non-finite values.
Results may differ from a plain program's by a relative error of at most 0.0062.
Values may be sent and summed in bfloat16 or wider, within the bound.
No kernel may reach another device: no remote copies, remote signals or barrier semaphores. Data moves between devices by JAX's collectives and lax.ppermute only.
A program may use at most 64 MiB of HBM per device.

v0:
```python
import functools

import jax
import jax.numpy as jnp
from jax import lax
from jax.experimental import pallas as pl
from jax.experimental.pallas import tpu as pltpu
from jax.sharding import PartitionSpec as P

CAP = 8
SOFTMAX_HEAT = 0.01
ADAPTER_SCALE = 2.0
EPSILON = 1e-06
LOWEST = -1e30
ID_BASE = 256
TOP_ROW, SUM_ROW, DOT_ROW, HEAD_ROWS = 8, 9, 10, 16
VMEM_BYTES = 16 * 1024 * 1024
PASSAGE_CHUNKS = 4
F32 = jnp.float32
BF16 = jnp.bfloat16


def dot_nn(a, b, precision=None):
    return lax.dot_general(
        a, b, (((1,), (0,)), ((), ())), precision=precision, preferred_element_type=F32
    )


def dot_nt(a, b, precision=None):
    return lax.dot_general(
        a, b, (((1,), (1,)), ((), ())), precision=precision, preferred_element_type=F32
    )


def split_two(values):
    high = values.astype(BF16)
    low = (values - high.astype(F32)).astype(BF16)
    return high, low


def dot_pieces(dot, a, b):
    rows = a.shape[0]
    a_high, a_low = split_two(a)
    b_high, b_low = split_two(b)
    both = dot(jnp.concatenate([a_high, a_low], axis=0), b_high)
    return both[:rows] + both[rows:] + dot(a_high, b_low)


def iota(shape, dim):
    return lax.broadcasted_iota(jnp.int32, shape, dim)


def shape_of(dims, kind):
    return jax.ShapeDtypeStruct(dims, kind)


def run(body, out_shape, args, flops, scratch=(), in_hbm=False):
    grant = VMEM_BYTES * max(1, size_ratio(args))
    if in_hbm:
        args = [pltpu.with_memory_space_constraint(a, pltpu.HBM) for a in args]
    vmem = pl.BlockSpec(memory_space=pltpu.VMEM)
    hbm = pl.BlockSpec(memory_space=pltpu.HBM)
    moved = sum(a.size * a.dtype.itemsize for a in (*args, *out_shape))
    return pl.pallas_call(
        body,
        out_shape=out_shape,
        in_specs=[hbm if in_hbm else vmem] * len(args),
        out_specs=tuple(vmem for _ in out_shape),
        scratch_shapes=list(scratch),
        compiler_params=pltpu.CompilerParams(vmem_limit_bytes=grant),
        cost_estimate=pl.CostEstimate(flops=flops, bytes_accessed=moved, transcendentals=0),
    )(*args)


def size_ratio(args):
    moved = sum(a.size * a.dtype.itemsize for a in args)
    return -(-moved * 3 // VMEM_BYTES)


def inverse_length(raw_ref, width):
    chunk = min(width, 512)
    total = jnp.zeros((raw_ref.shape[0], 1), F32)
    for at in range(0, width, chunk):
        part = raw_ref[:, at : at + chunk].astype(F32)
        total = total + jnp.sum(part * part, axis=-1, keepdims=True)
    return 1.0 / jnp.sqrt(total + EPSILON)


def front_kernel(
    query_ref,
    ids_ref,
    down_ref,
    up_ref,
    positive_ref,
    out_ref,
    adapter_ref,
    half_ref,
    tiled_ref,
    ids_here,
    positive_here,
    sems,
):
    width = query_ref.shape[1]
    rank = down_ref.shape[0]
    me = lax.axis_index("dp")
    pairs = (
        (ids_ref, ids_here),
        (query_ref, out_ref.at[:, pl.ds(0, width)]),
        (positive_ref, positive_here),
        (down_ref, adapter_ref.at[pl.ds(0, rank), :]),
        (up_ref, adapter_ref.at[pl.ds(rank, rank), :]),
    )
    copies = [pltpu.make_async_copy(a, b, sems.at[i]) for i, (a, b) in enumerate(pairs)]
    for copy in copies:
        copy.start()
    copies[0].wait()
    ids = ids_here[...]
    coded = jnp.concatenate([ids // ID_BASE, ids % ID_BASE], axis=1)
    out_ref[:, width:] = coded.astype(F32).astype(BF16)
    copies[2].wait()
    q_dev = positive_here.shape[1]
    for at in range(0, tiled_ref.shape[1], q_dev):
        tiled_ref[:, at : at + q_dev] = positive_here[...]
    copies[3].wait()
    copies[4].wait()

    @pl.when(me % 2 == 0)
    def _():
        half_ref[...] = adapter_ref[:rank, :]

    @pl.when(me % 2 == 1)
    def _():
        half_ref[...] = adapter_ref[rank:, :]

    copies[1].wait()


def passage_norm_kernel(
    passage_ref, home_ref, embed_ref, side_ref, row_ref, passage_here, home_here, sems
):
    rows, width = passage_ref.shape
    total = home_ref.shape[1]
    me = lax.axis_index("dp")
    part = rows // PASSAGE_CHUNKS
    home_copy = pltpu.make_async_copy(home_ref, home_here, sems.at[0])
    home_copy.start()
    passage_copies = []
    for c in range(PASSAGE_CHUNKS):
        here = pl.ds(c * part, part)
        passage_copies.append(
            pltpu.make_async_copy(
                passage_ref.at[here, :], passage_here.at[here, :], sems.at[1 + c]
            )
        )
        passage_copies[c].start()

    home_copy.wait()
    row_id = iota((rows, total), 0) + me * rows
    number = iota((rows, total), 1)
    home = jnp.where(home_here[...] == row_id, number, 0).astype(F32)
    home = jnp.sum(home, axis=1, keepdims=True)

    chunk = min(width, 512)
    inverses = []
    for c in range(PASSAGE_CHUNKS):
        passage_copies[c].wait()
        here = slice(c * part, (c + 1) * part)
        inverse = inverse_length(passage_here.at[here, :], width)
        for at in range(0, width, chunk):
            values = passage_here[here, at : at + chunk].astype(F32)
            embed_ref[here, at : at + chunk] = (values * inverse).astype(BF16)
        inverses.append(inverse)
    inverse = jnp.concatenate(inverses, axis=0)
    side_ref[...] = jnp.where(iota(side_ref.shape, 1) == 0, inverse, home)
    row_ref[...] = jnp.broadcast_to(inverse, (rows, rows)).T[: row_ref.shape[0]]


def stack_kernel(*refs):
    out_ref = refs[-1]
    rows = refs[0].shape[0]
    for i, ref in enumerate(refs[:-1]):
        out_ref[i * rows : (i + 1) * rows, :] = ref[...]


def stack(*parts):
    rows, cols = parts[0].shape
    return run(stack_kernel, (shape_of((len(parts) * rows, cols), parts[0].dtype),), parts, 1)[0]


def join_kernel(first_ref, second_ref, out_ref):
    rows = first_ref.shape[0]
    out_ref[:rows, :] = first_ref[...]
    out_ref[rows:, :] = second_ref[...]


def place_paired(own_ref, near_ref, far_ref, weights_ref):
    rank, part = own_ref.shape[0] // 2, own_ref.shape[1]
    me = lax.axis_index("fsdp")
    core = lax.axis_index("dp") % 2

    def columns(k):
        return pl.ds(pl.multiple_of((me ^ k) * part, part), part)

    def place(even_ref, odd_ref):
        weights_ref[:, columns(1)] = even_ref[: 2 * rank, :]
        weights_ref[:, columns(2)] = odd_ref[: 2 * rank, :]
        weights_ref[:rank, columns(3)] = even_ref[2 * rank :, :]
        weights_ref[rank:, columns(3)] = odd_ref[2 * rank :, :]

    weights_ref[:, columns(0)] = own_ref[...]
    pl.when(core == 0)(functools.partial(place, near_ref, far_ref))
    pl.when(core == 1)(functools.partial(place, far_ref, near_ref))


def place_blocks(*refs):
    part = refs[0].shape[1]
    me = lax.axis_index("fsdp")
    for k, ref in enumerate(refs[:-1]):
        refs[-1][:, pl.ds(pl.multiple_of((me ^ k) * part, part), part)] = ref[...]


def rank_kernel(shards, *refs):
    blocks = refs[:-12]
    query_ref, query_in_ref, passage_in_ref, embed_ref, row_ref = refs[-12:-7]
    onehot_ref, head_ref = refs[-7:-5]
    weights_ref, passage_low_ref, message_ref, own_ref, base_ref = refs[-5:]
    slots = onehot_ref.shape[0]
    rank = blocks[0].shape[0] // 2
    q_dev, width = query_ref.shape
    queries = own_ref.shape[1]
    place = place_paired if shards == 4 else place_blocks
    place(*blocks, weights_ref)
    down, up = weights_ref[:rank, :], weights_ref[rank:, :]
    start = lax.axis_index("dp") * q_dev
    place = iota((q_dev, queries), 1) == iota((q_dev, queries), 0) + start
    inverse = inverse_length(query_ref, width)
    own = jnp.sum(jnp.where(place, inverse, 0.0), axis=0, keepdims=True)
    own_ref[...] = jnp.broadcast_to(own, own_ref.shape)
    same = iota((q_dev, q_dev), 0) == iota((q_dev, q_dev), 1)
    inverse_row = jnp.sum(jnp.where(same, inverse, 0.0), axis=0, keepdims=True)
    query_low = dot_nt(down, query_in_ref[...]).astype(BF16)
    message_ref[HEAD_ROWS:, slots : slots + q_dev] = query_low.astype(F32) * inverse_row
    passage_low = dot_nt(down, passage_in_ref[...]).astype(BF16)
    passage_low_ref[...] = passage_low.astype(F32) * row_ref[0:1, :]
    base = dot_nt(up, embed_ref[...])
    base_ref[...] = base
    message_ref[:HEAD_ROWS, :] = head_ref[...]
    message_ref[HEAD_ROWS:, :slots] = dot_pieces(dot_nt, base, onehot_ref[...])
    unused = jnp.zeros((rank, queries - slots - q_dev), F32)
    message_ref[HEAD_ROWS:, slots + q_dev :] = unused


def score_kernel(group, *refs):
    blocks = refs[:group]
    embed_ref, side_ref, positive_ref = refs[group : group + 3]
    query_ref, weight_ref, dots_ref, onehot_ref, head_ref, coded_ref = refs[group + 3 :]
    rows, width = embed_ref.shape
    queries = query_ref.shape[0]
    q_dev = queries // group
    negatives = (blocks[0].shape[1] - width) // 2
    slots = group * CAP
    me = lax.axis_index("dp")
    chunk = min(width, 1024)
    for k in range(group):
        start = pl.multiple_of((me ^ k) * q_dev, q_dev)
        inverse = inverse_length(blocks[k], width)
        for at in range(0, width, chunk):
            part = blocks[k][:, at : at + chunk].astype(F32)
            query_ref[pl.ds(start, q_dev), at : at + chunk] = (part * inverse).astype(BF16)
        coded = blocks[k][:, width:].astype(F32)
        coded_ref[pl.ds(start, q_dev), :] = coded
    dots = dot_nt(embed_ref[...], query_ref[...])
    dots_ref[...] = dots
    scores = dots / SOFTMAX_HEAT

    coded = coded_ref[...].T
    ids = coded[:negatives] * float(ID_BASE) + coded[negatives:]
    home = jnp.broadcast_to(side_ref[:, 1:2], (rows, queries))
    count = jnp.zeros((rows, queries), F32)
    for j in range(negatives):
        count = count + jnp.where(ids[j : j + 1, :] == home, 1.0, 0.0)
    members = iota((slots, queries), 0) // CAP == iota((slots, queries), 1) // q_dev
    marked = dot_nt(members.astype(BF16), count.astype(BF16)) > 0.0
    before = (iota((rows, rows), 0) <= iota((rows, rows), 1)).astype(BF16)
    rank_in = dot_nn(marked.astype(F32).astype(BF16), before)
    wanted = (iota((slots, rows), 0) % CAP + 1).astype(F32)
    onehot = jnp.where(marked & (rank_in == wanted), 1.0, 0.0)
    onehot_ref[...] = onehot

    own = iota((rows, queries), 1) // q_dev == me
    count = count + jnp.where(own & (positive_ref[...] == iota((rows, queries), 0)), 1.0, 0.0)
    named = count > 0.0
    top = jnp.max(jnp.where(named, scores, LOWEST), axis=0, keepdims=True)
    weight = count * jnp.exp(jnp.where(named, scores - top, LOWEST))
    weight_ref[...] = weight
    total = jnp.sum(weight, axis=0, keepdims=True)
    dot_total = jnp.sum(weight * dots, axis=0, keepdims=True)
    slot_weight = dot_pieces(dot_nn, onehot, weight)
    tail_row = iota((HEAD_ROWS - CAP, queries), 0)
    tail = jnp.where(tail_row == 0, top, jnp.where(tail_row == 1, total, dot_total))
    lane_group = iota((CAP, queries), 1) // q_dev
    compact = jnp.zeros((CAP, queries), F32)
    for peer in range(group):
        part = slot_weight[peer * CAP : (peer + 1) * CAP]
        compact = jnp.where(lane_group == peer, part, compact)
    head_ref[:CAP, :] = compact
    head_ref[CAP:, :] = tail


def request_kernel(group, *refs):
    (
        embed_ref,
        onehot_ref,
        query_ref,
        weights_ref,
        low_ref,
        base_ref,
        weight_ref,
        positive_ref,
        back_ref,
        local_ref,
        target_ref,
    ) = refs[:11]
    blocks = refs[11:]
    width = embed_ref.shape[1]
    rows, queries = weight_ref.shape
    me = lax.axis_index("dp")
    onehot = [
        onehot_ref[pl.ds(pl.multiple_of((me ^ k) * CAP, CAP), CAP), :] for k in range(group)
    ]
    onehot = jnp.concatenate(onehot, axis=0).astype(BF16)
    chunk = min(width, 1024)
    for at in range(0, width, chunk):
        part = dot_nn(onehot, embed_ref[:, at : at + chunk]).astype(BF16)
        for i, block in enumerate(blocks):
            block[:, at : at + chunk] = part[2 * i * CAP : 2 * (i + 1) * CAP]
    back_ref[...] = dot_nt(weights_ref[weights_ref.shape[0] // 2 :, :], query_ref[...])
    both = jnp.concatenate([low_ref[...], base_ref[...]], axis=0)
    local_ref[...] = dot_pieces(dot_nn, both, weight_ref[...])
    target = own_target(positive_ref, rows, queries, queries // group, me)
    target_ref[...] = dot_pieces(dot_nn, both, target)


def forward_kernel(*refs):
    halves = [ref[...].astype(F32)[CAP:] for ref in refs[:-1]]
    refs[-1][...] = jnp.concatenate(halves, axis=0).astype(BF16)


def message_parts(near_ref, far_ref, group):
    rows = near_ref.shape[0] // (group // 2)
    return [((near_ref, far_ref)[k % 2], k // 2 * rows) for k in range(group)]


def combine(parts):
    tops = [ref[at + TOP_ROW : at + TOP_ROW + 1, :] for ref, at in parts]
    sums = [ref[at + SUM_ROW : at + SUM_ROW + 1, :] for ref, at in parts]
    top = functools.reduce(jnp.maximum, tops)
    scales = [jnp.exp(t - top) for t in tops]
    inverse_total = 1.0 / sum(t * s for t, s in zip(scales, sums))
    return [scale * inverse_total for scale in scales]


def own_target(positive_ref, rows, queries, q_dev, me):
    own = iota((rows, queries), 1) // q_dev == me
    return jnp.where(own & (positive_ref[...] == iota((rows, queries), 0)), 1.0, 0.0)


def terms_kernel(group, shards, near_ref, far_ref, *refs):
    parts = message_parts(near_ref, far_ref, group)
    (
        weight_ref,
        dots_ref,
        positive_ref,
        query_ref,
        embed_ref,
        back_query_ref,
        back_passage_ref,
        passage_low_ref,
        row_ref,
        own_ref,
        passage_in_ref,
        query_in_ref,
        local_ref,
        target_ref,
    ) = refs[:14]
    final_ref = refs[14]
    blocks = refs[15 : 15 + shards]
    (sum_ref,) = refs[15 + shards :]
    rows, queries = weight_ref.shape
    q_dev = queries // group
    rank = passage_low_ref.shape[0]
    width = query_ref.shape[1]
    me = lax.axis_index("dp")

    scales = combine(parts)
    target = own_target(positive_ref, rows, queries, q_dev, me)
    weight = (weight_ref[...] * scales[0] - target) / SOFTMAX_HEAT
    final_ref[...] = weight
    dots = dots_ref[...]
    ones = jnp.ones((16, queries), F32)
    inner = dot_pieces(dot_nt, ones, weight * dots)[0:1, :]

    inner_query = -jnp.sum(target * dots, axis=0, keepdims=True)
    own_dots = near_ref[DOT_ROW : DOT_ROW + 1, :]
    share = (scales[0] * own_dots + inner_query) / SOFTMAX_HEAT
    slots = group * CAP
    bases, query_low = [], []
    for (ref, at), scale in zip(parts, scales):
        inner_query = inner_query + scale * ref[at + DOT_ROW : at + DOT_ROW + 1, :]
        bases.append(ref[at + HEAD_ROWS : at + HEAD_ROWS + rank, :])
        query_low.append(ref[at + HEAD_ROWS : at + HEAD_ROWS + rank, :])
    low_total = jnp.zeros((rank, queries), F32)
    lane_group = iota((rank, queries), 1) // q_dev
    for k, rows_at in enumerate(query_low):
        shift = lax.rem((me ^ k) * q_dev + queries - slots, queries)
        rolled = pltpu.roll(rows_at, shift, 1)
        low_total = low_total + jnp.where(lane_group == (me ^ k), rolled, 0.0)
    query_low = low_total
    shift = lax.rem(queries - me * CAP, queries)
    bases = pltpu.roll(jnp.concatenate(bases[1:], axis=0), shift, 1)[:, :CAP]
    far_base = [bases[k * rank : (k + 1) * rank] for k in range(group - 1)]
    far_weight = [
        ref[at : at + CAP, :] * (scale / SOFTMAX_HEAT)
        for (ref, at), scale in zip(parts[1:], scales[1:])
    ]
    inner_query = inner_query / SOFTMAX_HEAT

    passage_low = passage_low_ref[...]
    local = (local_ref[...] * scales[0] - target_ref[...]) / SOFTMAX_HEAT
    from_query = local[:rank] - query_low * share
    from_passage = dot_pieces(dot_nt, query_low, weight) - passage_low * inner
    query_parts = jnp.concatenate(split_two(from_query), axis=0)
    passage_parts = jnp.concatenate(split_two(from_passage), axis=0)

    back_passage = dot_pieces(dot_nt, back_query_ref[...], weight)
    back_passage = (back_passage - back_passage_ref[...] * inner) * row_ref[0:1, :]
    back_passage = back_passage.astype(BF16)
    back_query = local[rank:] + dot_pieces(
        dot_nn, jnp.concatenate(far_base, axis=1), jnp.concatenate(far_weight, axis=0)
    )
    back_query = (back_query - back_query_ref[...] * inner_query) * own_ref[0:1, :]
    pick = (iota((q_dev, queries), 1) == iota((q_dev, queries), 0) + me * q_dev).astype(BF16)
    back_query = dot_nt(back_query.astype(BF16), pick).astype(BF16)

    chunk = min(width, 512)
    for at in range(0, width, chunk):
        cols = slice(at, at + chunk)
        both = dot_nn(query_parts, query_ref[:, cols]) + dot_nn(passage_parts, embed_ref[:, cols])
        sum_ref[rank:, cols] = ADAPTER_SCALE * (both[:rank] + both[rank:])
        sum_ref[:rank, cols] = ADAPTER_SCALE * (
            dot_nn(back_passage, passage_in_ref[:, cols])
            + dot_nn(back_query, query_in_ref[:, cols])
        )
    part = width // shards
    home = lax.axis_index("fsdp")
    for k in range(shards):
        start = pl.multiple_of((home ^ k) * part, part)
        blocks[k][...] = sum_ref[:, pl.ds(start, part)].astype(blocks[k].dtype)


def backward(upstream_of, raw_ref, inverse, grad_ref, up_ref):
    rows, width = raw_ref.shape
    chunk = min(width, 512)
    inner = jnp.zeros((rows, 1), F32)
    for at in range(0, width, chunk):
        upstream = upstream_of(at, chunk)
        up_ref[:, at : at + chunk] = upstream
        unit = raw_ref[:, at : at + chunk].astype(F32) * inverse
        inner = inner + jnp.sum(unit * upstream, axis=-1, keepdims=True)
    for at in range(0, width, chunk):
        unit = raw_ref[:, at : at + chunk].astype(F32) * inverse
        grad = (up_ref[:, at : at + chunk] - unit * inner) * inverse
        grad_ref[:, at : at + chunk] = grad.astype(BF16)


def passage_kernel(final_ref, query_ref, raw_ref, side_ref, grad_ref, up_ref):
    high, low = split_two(final_ref[...])

    def upstream_of(at, chunk):
        embed = query_ref[:, at : at + chunk]
        return dot_nn(high, embed) + dot_nn(low, embed)

    backward(upstream_of, raw_ref, side_ref[:, 0:1], grad_ref, up_ref)


def query_kernel(group, near_ref, far_ref, *refs):
    parts = message_parts(near_ref, far_ref, group)
    near = refs[: group // 2 - 1]
    forwarded_ref, final_ref, embed_ref, raw_ref, grad_ref, up_ref = refs[group // 2 - 1 :]
    q_dev, width = raw_ref.shape
    queries = final_ref.shape[1]
    me = lax.axis_index("dp")
    scales = combine(parts)
    pick = (iota((q_dev, queries), 1) == iota((q_dev, queries), 0) + me * q_dev).astype(F32)
    far = [
        ref[at : at + CAP, :] * (scale / SOFTMAX_HEAT) for (ref, at), scale in zip(parts, scales)
    ]
    far = far[2::2] + far[1::2] + [jnp.zeros((CAP, queries), F32)]
    own_parts = split_two(dot_pieces(dot_nt, pick, final_ref[...]))
    far_parts = split_two(dot_pieces(dot_nt, pick, jnp.concatenate(far, axis=0)))
    own_parts = jnp.concatenate(own_parts, axis=0)
    far_parts = jnp.concatenate(far_parts, axis=0)

    def upstream_of(at, chunk):
        rows = [ref[:, at : at + chunk].astype(F32)[:CAP] for ref in near]
        rows.append(forwarded_ref[:, at : at + chunk].astype(F32))
        rows.append(jnp.zeros((CAP, chunk), F32))
        both = dot_nn(own_parts, embed_ref[:, at : at + chunk])
        both = both + dot_nn(far_parts, jnp.concatenate(rows, axis=0).astype(BF16))
        return both[:q_dev] + both[q_dev:]

    backward(upstream_of, raw_ref, inverse_length(raw_ref, width), grad_ref, up_ref)


def sum_kernel(*refs):
    total = refs[0][...].astype(F32)
    for ref in refs[1:-1]:
        total = total + ref[...].astype(F32)
    refs[-1][...] = total


def sum_two_kernel(left_ref, right_ref, sent_ref):
    sent_ref[...] = (left_ref[...] + right_ref[...]).astype(BF16)


def sum_split_kernel(*refs):
    terms = [ref[...].astype(F32) for ref in refs[:-2]]
    while len(terms) > 1:
        terms = [a + b for a, b in zip(terms[::2], terms[1::2])]
    rank = refs[-1].shape[0]
    refs[-2][...] = terms[0][:rank]
    refs[-1][...] = terms[0][rank:]


def exchange(values, axis, k):
    size = lax.axis_size(axis)
    return lax.ppermute(values, axis, [(i, i ^ k) for i in range(size)])


def core_step(values, even_step, odd_step):
    outer, inner = lax.axis_size("dp"), lax.axis_size("fsdp")
    pairs = []
    for d in range(outer):
        step = odd_step if d % 2 else even_step
        pairs += [(d * inner + f, d * inner + (f ^ step)) for f in range(inner)]
    return lax.ppermute(values, ("dp", "fsdp"), pairs)


def per_device(
    query_pooled_states,
    passage_pooled_states,
    query_attention_output,
    passage_attention_output,
    positive_passage_row,
    hard_negative_ids,
    passage_home_row,
    adapter_down_weight,
    adapter_up_weight,
):
    group = lax.axis_size("dp")
    shards = lax.axis_size("fsdp")
    query_raw = query_pooled_states[0]
    passage_raw = passage_pooled_states[0]
    query_in = query_attention_output[0]
    passage_in = passage_attention_output[0]
    ids = hard_negative_ids[0]
    q_dev, width = query_raw.shape
    p_dev = passage_raw.shape[0]
    rank, part = adapter_down_weight.shape
    queries = group * q_dev
    slots = group * CAP
    work = 2 * p_dev * width

    packed, adapter, half, positive_row = run(
        front_kernel,
        (
            shape_of((q_dev, width + 2 * ids.shape[1]), BF16),
            shape_of((2 * rank, part), BF16),
            shape_of((rank, part), BF16),
            shape_of((1, queries), jnp.int32),
        ),
        (query_raw, ids, adapter_down_weight, adapter_up_weight, positive_passage_row),
        1,
        [
            pltpu.VMEM(ids.shape, jnp.int32),
            pltpu.VMEM(positive_passage_row.shape, jnp.int32),
            pltpu.SemaphoreType.DMA((5,)),
        ],
        in_hbm=True,
    )
    embed, side, side_row = run(
        passage_norm_kernel,
        (
            shape_of((p_dev, width), BF16),
            shape_of((p_dev, 128), F32),
            shape_of((8, p_dev), F32),
        ),
        (passage_raw, passage_home_row),
        work,
        [
            pltpu.VMEM(passage_raw.shape, BF16),
            pltpu.VMEM(passage_home_row.shape, jnp.int32),
            pltpu.SemaphoreType.DMA((1 + PASSAGE_CHUNKS,)),
        ],
        in_hbm=True,
    )
    blocks = {0: packed}
    for k in range(2, group, 2):
        blocks[k] = exchange(packed, "dp", k)
    blocks[1] = exchange(packed, "dp", 1)
    for k in range(2, group, 2):
        blocks[k], embed = lax.optimization_barrier((blocks[k], embed))
        blocks[k ^ 1] = exchange(blocks[k], "dp", 1)
    if shards == 4:
        half_block = exchange(half, "fsdp", 3)
        whole_block = core_step(adapter, 1, 2)
        adapter_near = run(
            join_kernel,
            (shape_of((3 * rank, part), BF16),),
            (whole_block, half_block),
            1,
        )[0]
        adapter_blocks = [adapter, adapter_near, exchange(adapter_near, "dp", 1)]
    else:
        adapter_blocks = [adapter] + [exchange(adapter, "fsdp", k) for k in range(1, shards)]
    query_embed, weight, dots, onehot, head = run(
        functools.partial(score_kernel, group),
        (
            shape_of((queries, width), BF16),
            shape_of((p_dev, queries), F32),
            shape_of((p_dev, queries), F32),
            shape_of((slots, p_dev), F32),
            shape_of((HEAD_ROWS, queries), F32),
        ),
        (
            *[blocks[k] for k in range(group)],
            embed,
            side,
            positive_row,
        ),
        work * queries,
        [pltpu.VMEM((queries, 2 * ids.shape[1]), F32)],
    )
    adapter_full, passage_low, message, own_side, slot_base = run(
        functools.partial(rank_kernel, shards),
        (
            shape_of((2 * rank, width), BF16),
            shape_of((rank, p_dev), F32),
            shape_of((HEAD_ROWS + rank, queries), F32),
            shape_of((8, queries), F32),
            shape_of((rank, p_dev), F32),
        ),
        (
            *adapter_blocks,
            query_raw,
            query_in,
            passage_in,
            embed,
            side_row,
            onehot,
            head,
        ),
        work * rank,
    )
    stats = [message] + [exchange(message, "dp", k) for k in range(2, group, 2)]
    chips = group // 2
    back_query, local, targets, *row_blocks = run(
        functools.partial(request_kernel, group),
        (
            shape_of((rank, queries), F32),
            shape_of((2 * rank, queries), F32),
            shape_of((2 * rank, queries), F32),
            *[shape_of((2 * CAP, width), BF16)] * chips,
        ),
        (
            embed,
            onehot,
            query_embed,
            adapter_full,
            passage_low,
            slot_base,
            weight,
            positive_row,
        ),
        work * slots,
    )
    stats, row_blocks = lax.optimization_barrier((stats, row_blocks))
    near = [exchange(row_blocks[i], "dp", 2 * i) for i in range(1, chips)]
    near_stats = stack(*stats)
    far_stats = exchange(near_stats, "dp", 1)
    final, *terms = run(
        functools.partial(terms_kernel, group, shards),
        (
            shape_of((p_dev, queries), F32),
            shape_of((2 * rank, part), F32),
            *[shape_of((2 * rank, part), BF16)] * (shards - 1),
        ),
        (
            near_stats,
            far_stats,
            weight,
            dots,
            positive_row,
            query_embed,
            embed,
            back_query,
            slot_base,
            passage_low,
            side_row,
            own_side,
            passage_in,
            query_in,
            local,
            targets,
        ),
        work * rank * 4,
        [pltpu.VMEM((2 * rank, width), F32)],
    )
    arrived = [exchange(terms[k], "fsdp", k) for k in range(1, shards)]
    final, near[0] = lax.optimization_barrier((final, near[0]))
    grad_passage = run(
        passage_kernel,
        (shape_of((p_dev, width), BF16),),
        (final, query_embed, passage_raw, side),
        2 * work * queries,
        [pltpu.VMEM((p_dev, width), F32)],
    )[0]
    terms[0], grad_passage = lax.optimization_barrier((terms[0], grad_passage))
    total = run(sum_kernel, (shape_of((2 * rank, part), F32),), (terms[0], *arrived), 1)[0]
    total, near = lax.optimization_barrier((total, near))
    to_sibling = run(
        forward_kernel,
        (shape_of((group // 2 * CAP, width), BF16),),
        (row_blocks[0], *near),
        1,
    )[0]
    forwarded = exchange(to_sibling, "dp", 1)
    sent = run(
        sum_two_kernel,
        (shape_of((2 * rank, part), BF16),),
        (total, exchange(total, "dp", 1)),
        1,
    )[0]
    arrived = [exchange(sent, "dp", k) for k in range(2, group, 2)]
    grad_query = run(
        functools.partial(query_kernel, group),
        (shape_of((q_dev, width), BF16),),
        (near_stats, far_stats, *near, forwarded, final, embed, query_raw),
        4 * q_dev * width * (p_dev + slots),
        [pltpu.VMEM((q_dev, width), F32)],
    )[0]
    sent, grad_query = lax.optimization_barrier((sent, grad_query))
    down_total, up_total = run(
        sum_split_kernel, (shape_of((rank, part), F32),) * 2, (sent, *arrived), 1
    )
    return (grad_query[None], grad_passage[None], down_total, up_total)


def solution(mesh):
    in_specs = (
        P("fsdp", "dp", None),
        P("fsdp", "dp", None),
        P("fsdp", "dp", None),
        P("fsdp", "dp", None),
        P("fsdp", "dp"),
        P("fsdp", "dp", None),
        P("fsdp", None),
        P(None, "fsdp"),
        P(None, "fsdp"),
    )
    out_specs = (P("fsdp", "dp", None), P("fsdp", "dp", None), P(None, "fsdp"), P(None, "fsdp"))
    return jax.shard_map(
        per_device, mesh=mesh, in_specs=in_specs, out_specs=out_specs, check_vma=False
    )
```

profile of v0, /device:TPU:0, one launch (start us, length us, event | category | flops | bytes accessed | tf_op | source)
XLA Modules:
  0.0 47.4 jit_solution(3166205850043030336)
XLA Ops:
  0.6 1.0 %shard_map.120 = (bf16[16,4224]{1,0:T(8,128)(2,1)S(1)}, bf16[32,1024]{1,0:T(8,128)(2,1)S(1)}, bf16[16,1024]{1,0:T(8,128)(2,1)S(1)}, s32[1,128]{1,0:T(1,128)S(1)}) custom-call(bf16[16,4096]{1,0:T(8,128)(2,1)} %bitcast.11, s32[16,64]{1,0:T(8,128)} %bitcast.18, bf16[16,1024]{1,0:T(8,128)(2,1)} %down_ref.1, bf16[16,1024]{1,0:T(8,128)(2,1)} %up_ref.1, ...), custom_call_target="tpu_custom_call" | custom-call | flops 1 | bytes 434752 | tf_op jit(solution)/shard_map/pallas_call | solution.py:64
  1.6 3.0 %collective-permute-start.5 = (bf16[16,4224]{1,0:T(8,128)(2,1)S(1)}, bf16[16,4224]{1,0:T(8,128)(2,1)S(1)}, u32[]{:S(2)}, u32[]{:S(2)}) collective-permute-start(bf16[16,4224]{1,0:T(8,128)(2,1)S(1)} %get-tuple-element.61.refs_0_), channel_id=1, source_target_pairs={{0,8},{4,12},{8,0},{12,4},{16,24},{20,28},{24,16},{28,20},{1,9},{5... | collective-permute-start | bytes 405512 | tf_op jit(solution)/shard_map/ppermute | solution.py:537
  4.6 1.5 %collective-permute-start.4 = (bf16[16,4224]{1,0:T(8,128)(2,1)S(1)}, bf16[16,4224]{1,0:T(8,128)(2,1)S(1)}, u32[]{:S(2)}, u32[]{:S(2)}) collective-permute-start(bf16[16,4224]{1,0:T(8,128)(2,1)S(1)} %get-tuple-element.61.refs_0_), channel_id=1, source_target_pairs={{0,16},{4,20},{8,24},{12,28},{16,0},{20,4},{24,8},{28,12},{1,17},{... | collective-permute-start | bytes 405512 | tf_op jit(solution)/shard_map/ppermute | solution.py:537
  6.2 4.1 %collective-permute-start.1 = (bf16[16,1024]{1,0:T(8,128)(2,1)S(1)}, bf16[16,1024]{1,0:T(8,128)(2,1)S(1)}, u32[]{:S(2)}, u32[]{:S(2)}) collective-permute-start(bf16[16,1024]{1,0:T(8,128)(2,1)S(1)} %get-tuple-element.60), channel_id=1, source_target_pairs={{0,3},{1,2},{2,1},{3,0},{4,7},{5,6},{6,5},{7,4},{8,11},{9,10},{10,... | collective-permute-start | bytes 98312 | tf_op jit(solution)/shard_map/ppermute | solution.py:537
  10.2 1.8 %shard_map.122 = (bf16[128,4096]{1,0:T(8,128)(2,1)S(1)}, f32[128,128]{1,0:T(8,128)S(1)}, f32[8,128]{1,0:T(8,128)S(1)}) custom-call(bf16[128,4096]{1,0:T(8,128)(2,1)} %bitcast.7, s32[1,1024]{1,0:T(1,128)} %home_ref.1), custom_call_target="tpu_custom_call" | custom-call | flops 1048576 | bytes 2170880 | tf_op jit(solution)/shard_map/pallas_call | solution.py:64
  13.1 1.4 %collective-permute-done.first_ref = bf16[32,1024]{1,0:T(8,128)(2,1)S(1)} collective-permute-done((bf16[32,1024]{1,0:T(8,128)(2,1)S(1)}, bf16[32,1024]{1,0:T(8,128)(2,1)S(1)}, u32[]{:S(2)}, u32[]{:S(2)}) %collective-permute-start) | collective-permute-done | bytes 65568 | tf_op jit(solution)/shard_map/ppermute | solution.py:546
  14.6 1.4 %shard_map.123 = (bf16[128,4096]{1,0:T(8,128)(2,1)S(1)}, f32[128,128]{1,0:T(8,128)S(1)}, f32[128,128]{1,0:T(8,128)S(1)}, f32[64,128]{1,0:T(8,128)S(1)}, f32[16,128]{1,0:T(8,128)S(1)}) custom-call(bf16[16,4224]{1,0:T(8,128)(2,1)S(1)} %get-tuple-element.61.refs_0_, bf16[16,4224]{1,0:T(8,128)(2,1)S(1)} %collective-permute-done.6.refs_1_, ...), custom_call_target="tpu_custom_call" | custom-call | flops 134217728 | bytes 3416576 | tf_op jit(solution)/shard_map/pallas_call | solution.py:64
  16.1 0.9 %shard_map.124 = (bf16[32,4096]{1,0:T(8,128)(2,1)S(1)}, f32[16,128]{1,0:T(8,128)S(1)}, f32[32,128]{1,0:T(8,128)S(1)}, f32[8,128]{1,0:T(8,128)S(1)}, f32[16,128]{1,0:T(8,128)S(1)}) custom-call(bf16[32,1024]{1,0:T(8,128)(2,1)S(1)} %get-tuple-element.59.refs_0_, bf16[48,1024]{1,0:T(8,128)(2,1)S(1)} %shard_map.121.refs_1_, ...), custom_call_target="tpu_custom_call" | custom-call | flops 16777216 | bytes 2965504 | tf_op jit(solution)/shard_map/pallas_call | solution.py:64
  17.0 2.5 %collective-permute-start.12 = (f32[32,128]{1,0:T(8,128)S(1)}, f32[32,128]{1,0:T(8,128)S(1)}, u32[]{:S(2)}, u32[]{:S(2)}) collective-permute-start(f32[32,128]{1,0:T(8,128)S(1)} %get-tuple-element.84.refs_0_), channel_id=1, source_target_pairs={{0,24},{4,28},{8,16},{12,20},{16,8},{20,12},{24,0},{28,4},{1,25},{... | collective-permute-start | bytes 49160 | tf_op jit(solution)/shard_map/ppermute | solution.py:537
  19.5 0.5 %collective-permute-start.11 = (f32[32,128]{1,0:T(8,128)S(1)}, f32[32,128]{1,0:T(8,128)S(1)}, u32[]{:S(2)}, u32[]{:S(2)}) collective-permute-start(f32[32,128]{1,0:T(8,128)S(1)} %get-tuple-element.84.refs_0_), channel_id=1, source_target_pairs={{0,16},{4,20},{8,24},{12,28},{16,0},{20,4},{24,8},{28,12},{1,17},{... | collective-permute-start | bytes 49160 | tf_op jit(solution)/shard_map/ppermute | solution.py:537
  20.0 0.5 %collective-permute-start.10 = (f32[32,128]{1,0:T(8,128)S(1)}, f32[32,128]{1,0:T(8,128)S(1)}, u32[]{:S(2)}, u32[]{:S(2)}) collective-permute-start(f32[32,128]{1,0:T(8,128)S(1)} %get-tuple-element.84.refs_0_), channel_id=1, source_target_pairs={{0,8},{4,12},{8,0},{12,4},{16,24},{20,28},{24,16},{28,20},{1,9},{5... | collective-permute-start | bytes 49160 | tf_op jit(solution)/shard_map/ppermute | solution.py:537
  20.5 0.5 %shard_map.125 = (f32[16,128]{1,0:T(8,128)S(1)}, f32[32,128]{1,0:T(8,128)S(1)}, f32[32,128]{1,0:T(8,128)S(1)}, bf16[16,4096]{1,0:T(8,128)(2,1)S(1)}, bf16[16,409...) custom-call(bf16[128,4096]{1,0:T(8,128)(2,1)S(1)} %get-tuple-element.65.refs_8_.refs_6_.refs_0_.refs_4_, ...), custom_call_target="tpu_custom_call" | custom-call | flops 67108864 | bytes 3039744 | tf_op jit(solution)/shard_map/pallas_call | solution.py:64
  21.1 0.6 %collective-permute-done.12.refs_3_ = f32[32,128]{1,0:T(8,128)S(1)} collective-permute-done((f32[32,128]{1,0:T(8,128)S(1)}, f32[32,128]{1,0:T(8,128)S(1)}, u32[]{:S(2)}, u32[]{:S(2)}) %collective-permute-start.12) | collective-permute-done | bytes 16416 | tf_op jit(solution)/shard_map/ppermute | solution.py:537
  21.7 1.5 %collective-permute-done.11.refs_2_ = f32[32,128]{1,0:T(8,128)S(1)} collective-permute-done((f32[32,128]{1,0:T(8,128)S(1)}, f32[32,128]{1,0:T(8,128)S(1)}, u32[]{:S(2)}, u32[]{:S(2)}) %collective-permute-start.11) | collective-permute-done | bytes 16416 | tf_op jit(solution)/shard_map/ppermute | solution.py:537
  23.2 0.5 %collective-permute-done.10.refs_1_ = f32[32,128]{1,0:T(8,128)S(1)} collective-permute-done((f32[32,128]{1,0:T(8,128)S(1)}, f32[32,128]{1,0:T(8,128)S(1)}, u32[]{:S(2)}, u32[]{:S(2)}) %collective-permute-start.10) | collective-permute-done | bytes 16416 | tf_op jit(solution)/shard_map/ppermute | solution.py:537
  23.7 0.5 %collective-permute-start.14 = (bf16[16,4096]{1,0:T(8,128)(2,1)S(1)}, bf16[16,4096]{1,0:T(8,128)(2,1)S(1)}, u32[]{:S(2)}, u32[]{:S(2)}) collective-permute-start(bf16[16,4096]{1,0:T(8,128)(2,1)S(1)} %get-tuple-element.95), channel_id=1, source_target_pairs={{0,8},{4,12},{8,0},{12,4},{16,24},{20,28},{24,16},{28,20},{1,9},{5... | collective-permute-start | bytes 393224 | tf_op jit(solution)/shard_map/ppermute | solution.py:537
  24.3 1.6 %collective-permute-start.18 = (bf16[16,4096]{1,0:T(8,128)(2,1)S(1)}, bf16[16,4096]{1,0:T(8,128)(2,1)S(1)}, u32[]{:S(2)}, u32[]{:S(2)}) collective-permute-start(bf16[16,4096]{1,0:T(8,128)(2,1)S(1)} %get-tuple-element.102), channel_id=1, source_target_pairs={{0,16},{4,20},{8,24},{12,28},{16,0},{20,4},{24,8},{28,12},{1,17},{... | collective-permute-start | bytes 393224 | tf_op jit(solution)/shard_map/ppermute | solution.py:537
  25.9 1.4 %collective-permute-start.19 = (bf16[16,4096]{1,0:T(8,128)(2,1)S(1)}, bf16[16,4096]{1,0:T(8,128)(2,1)S(1)}, u32[]{:S(2)}, u32[]{:S(2)}) collective-permute-start(bf16[16,4096]{1,0:T(8,128)(2,1)S(1)} %get-tuple-element.103), channel_id=1, source_target_pairs={{0,24},{4,28},{8,16},{12,20},{16,8},{20,12},{24,0},{28,4},{1,25},{... | collective-permute-start | bytes 393224 | tf_op jit(solution)/shard_map/ppermute | solution.py:537
  27.3 1.0 %shard_map.127 = (f32[128,128]{1,0:T(8,128)S(1)}, f32[32,1024]{1,0:T(8,128)S(1)}, bf16[32,1024]{1,0:T(8,128)(2,1)S(1)}, bf16[32,1024]{1,0:T(8,128)(2,1)S(1)}, bf16[32,1024]{1,0:T(8,128)(2,1)S(1)}) custom-call(f32[128,128]{1,0:T(8,128)S(1)} %shard_map.126.near_ref, f32[128,128]{1,0:T(8,128)S(1)} %collective-permute-done.13.far_ref, ...), custom_call_target="tpu_custom_call" | custom-call | flops 67108864 | bytes 3998208 | tf_op jit(solution)/shard_map/pallas_call | solution.py:64
  28.3 1.6 %collective-permute-start.15 = (bf16[32,1024]{1,0:T(8,128)(2,1)S(1)}, bf16[32,1024]{1,0:T(8,128)(2,1)S(1)}, u32[]{:S(2)}, u32[]{:S(2)}) collective-permute-start(bf16[32,1024]{1,0:T(8,128)(2,1)S(1)} %get-tuple-element.98), channel_id=1, source_target_pairs={{0,1},{1,0},{2,3},{3,2},{4,5},{5,4},{6,7},{7,6},{8,9},{9,8},{10,11... | collective-permute-start | bytes 196616 | tf_op jit(solution)/shard_map/ppermute | solution.py:537
  29.9 2.2 %collective-permute-start.16 = (bf16[32,1024]{1,0:T(8,128)(2,1)S(1)}, bf16[32,1024]{1,0:T(8,128)(2,1)S(1)}, u32[]{:S(2)}, u32[]{:S(2)}) collective-permute-start(bf16[32,1024]{1,0:T(8,128)(2,1)S(1)} %get-tuple-element.99), channel_id=1, source_target_pairs={{0,2},{1,3},{2,0},{3,1},{4,6},{5,7},{6,4},{7,5},{8,10},{9,11},{10,... | collective-permute-start | bytes 196616 | tf_op jit(solution)/shard_map/ppermute | solution.py:537
  32.1 0.7 %collective-permute-start.17 = (bf16[32,1024]{1,0:T(8,128)(2,1)S(1)}, bf16[32,1024]{1,0:T(8,128)(2,1)S(1)}, u32[]{:S(2)}, u32[]{:S(2)}) collective-permute-start(bf16[32,1024]{1,0:T(8,128)(2,1)S(1)} %get-tuple-element.100), channel_id=1, source_target_pairs={{0,3},{1,2},{2,1},{3,0},{4,7},{5,6},{6,5},{7,4},{8,11},{9,10},{10,... | collective-permute-start | bytes 196616 | tf_op jit(solution)/shard_map/ppermute | solution.py:537
  32.8 2.2 %shard_map.128 = bf16[128,4096]{1,0:T(8,128)(2,1)} custom-call(f32[128,128]{1,0:T(8,128)S(1)} %get-tuple-element.96.final_ref.refs_4_, bf16[128,4096]{1,0:T(8,128)(2,1)S(1)} %get-tuple-element.75.refs_2_.refs_3_.query_ref, bf16[128,4096]{1,0:T(8,128)(2,1)S(1)} %bitcast.8, f32[128,128]{1,0:T(8,128)S(1)} %get-tuple-element.70.refs_9_.side_ref), custom_call_target="tpu_custom_call" | custom-call | flops 268435456 | bytes 3276800 | tf_op jit(solution)/shard_map/pallas_call | solution.py:64
  35.0 2.3 %collective-permute-done.16.refs_2_ = bf16[32,1024]{1,0:T(8,128)(2,1)S(1)} collective-permute-done((bf16[32,1024]{1,0:T(8,128)(2,1)S(1)}, bf16[32,1024]{1,0:T(8,128)(2,1)S(1)}, u32[]{:S(2)}, u32[]{:S(2)}) %collective-permute-start.16) | collective-permute-done | bytes 65568 | tf_op jit(solution)/shard_map/ppermute | solution.py:537
  37.2 1.0 %collective-permute-done.17.refs_3_ = bf16[32,1024]{1,0:T(8,128)(2,1)S(1)} collective-permute-done((bf16[32,1024]{1,0:T(8,128)(2,1)S(1)}, bf16[32,1024]{1,0:T(8,128)(2,1)S(1)}, u32[]{:S(2)}, u32[]{:S(2)}) %collective-permute-start.17) | collective-permute-done | bytes 65568 | tf_op jit(solution)/shard_map/ppermute | solution.py:537
  38.9 1.2 %collective-permute-done.20.right_ref = f32[32,1024]{1,0:T(8,128)S(1)} collective-permute-done((f32[32,1024]{1,0:T(8,128)S(1)}, f32[32,1024]{1,0:T(8,128)S(1)}, u32[]{:S(2)}, u32[]{:S(2)}) %collective-permute-start.20) | collective-permute-done | bytes 131104 | tf_op jit(solution)/shard_map/ppermute | solution.py:537
  40.2 1.8 %collective-permute-start.24 = (bf16[32,1024]{1,0:T(8,128)(2,1)S(1)}, bf16[32,1024]{1,0:T(8,128)(2,1)S(1)}, u32[]{:S(2)}, u32[]{:S(2)}) collective-permute-start(bf16[32,1024]{1,0:T(8,128)(2,1)S(1)} %shard_map.130.refs_0_), channel_id=1, source_target_pairs={{0,24},{4,28},{8,16},{12,20},{16,8},{20,12},{24,0},{28,4},{1,25},{... | collective-permute-start | bytes 196616 | tf_op jit(solution)/shard_map/ppermute | solution.py:537
  42.0 0.5 %collective-permute-start.23 = (bf16[32,1024]{1,0:T(8,128)(2,1)S(1)}, bf16[32,1024]{1,0:T(8,128)(2,1)S(1)}, u32[]{:S(2)}, u32[]{:S(2)}) collective-permute-start(bf16[32,1024]{1,0:T(8,128)(2,1)S(1)} %shard_map.130.refs_0_), channel_id=1, source_target_pairs={{0,16},{4,20},{8,24},{12,28},{16,0},{20,4},{24,8},{28,12},{1,17},{... | collective-permute-start | bytes 196616 | tf_op jit(solution)/shard_map/ppermute | solution.py:537
  42.5 1.2 %collective-permute-start.22 = (bf16[32,1024]{1,0:T(8,128)(2,1)S(1)}, bf16[32,1024]{1,0:T(8,128)(2,1)S(1)}, u32[]{:S(2)}, u32[]{:S(2)}) collective-permute-start(bf16[32,1024]{1,0:T(8,128)(2,1)S(1)} %shard_map.130.refs_0_), channel_id=1, source_target_pairs={{0,8},{4,12},{8,0},{12,4},{16,24},{20,28},{24,16},{28,20},{1,9},{5... | collective-permute-start | bytes 196616 | tf_op jit(solution)/shard_map/ppermute | solution.py:537
  43.7 1.3 %shard_map.132 = bf16[16,4096]{1,0:T(8,128)(2,1)} custom-call(f32[128,128]{1,0:T(8,128)S(1)} %shard_map.126.near_ref, f32[128,128]{1,0:T(8,128)S(1)} %collective-permute-done.13.far_ref, bf16[16,4096]{1,0:T(8,128)(2,1)S(1)} %collective-permute-done.14.refs_1_.refs_0_, bf16[16,4096]{1,0:T(8,128)(2,1)S(1)} %collective-permute-done.18.refs_2_.refs_1_, ...), custom_call_target="tpu_custom_call" | custom-call | flops 50331648 | bytes 2162688 | tf_op jit(solution)/shard_map/pallas_call | solution.py:64
  45.5 1.2 %collective-permute-done.23.refs_2_ = bf16[32,1024]{1,0:T(8,128)(2,1)S(1)} collective-permute-done((bf16[32,1024]{1,0:T(8,128)(2,1)S(1)}, bf16[32,1024]{1,0:T(8,128)(2,1)S(1)}, u32[]{:S(2)}, u32[]{:S(2)}) %collective-permute-start.23) | collective-permute-done | bytes 65568 | tf_op jit(solution)/shard_map/ppermute | solution.py:537
  46.8 0.7 %shard_map.133 = (f32[16,1024]{1,0:T(8,128)}, f32[16,1024]{1,0:T(8,128)}) custom-call(bf16[32,1024]{1,0:T(8,128)(2,1)S(1)} %shard_map.130.refs_0_, bf16[32,1024]{1,0:T(8,128)(2,1)S(1)} %collective-permute-done.22.refs_1_, bf16[32,1024]{1,0:T(8,128)(2,1)S(1)} %collective-permute-done.23.refs_2_, bf16[32,1024]{1,0:T(8,128)(2,1)S(1)} %collective-permute-done.24.refs_3_), custom_call_target="tpu_custom_call" | custom-call | flops 1 | bytes 393216 | tf_op jit(solution)/shard_map/pallas_call | solution.py:64
  (40 shorter events, 2.4 us)
Async XLA Ops:
  1.6 10.4 %collective-permute-start.5 = (bf16[16,4224]{1,0:T(8,128)(2,1)S(1)}, bf16[16,4224]{1,0:T(8,128)(2,1)S(1)}, u32[]{:S(2)}, u32[]{:S(2)}) collective-permute-start(bf16[16,4224]{1,0:T(8,128)(2,1)S(1)} %get-tuple-element.61.refs_0_), channel_id=1, source_target_pairs={{0,8},{4,12},{8,0},{12,4},{16,24},{20,28},{24,16},{28,20},{1,9},{5... | collective-permute-start | bytes 405512 | tf_op jit(solution)/shard_map/ppermute | solution.py:537
  4.6 7.9 %collective-permute-start.4 = (bf16[16,4224]{1,0:T(8,128)(2,1)S(1)}, bf16[16,4224]{1,0:T(8,128)(2,1)S(1)}, u32[]{:S(2)}, u32[]{:S(2)}) collective-permute-start(bf16[16,4224]{1,0:T(8,128)(2,1)S(1)} %get-tuple-element.61.refs_0_), channel_id=1, source_target_pairs={{0,16},{4,20},{8,24},{12,28},{16,0},{20,4},{24,8},{28,12},{1,17},{... | collective-permute-start | bytes 405512 | tf_op jit(solution)/shard_map/ppermute | solution.py:537
  6.1 6.4 %collective-permute-start.3 = (bf16[16,4224]{1,0:T(8,128)(2,1)S(1)}, bf16[16,4224]{1,0:T(8,128)(2,1)S(1)}, u32[]{:S(2)}, u32[]{:S(2)}) collective-permute-start(bf16[16,4224]{1,0:T(8,128)(2,1)S(1)} %get-tuple-element.61.refs_0_), channel_id=1, source_target_pairs={{0,24},{4,28},{8,16},{12,20},{16,8},{20,12},{24,0},{28,4},{1,25},{... | collective-permute-start | bytes 405512 | tf_op jit(solution)/shard_map/ppermute | solution.py:537
  6.2 6.9 %collective-permute-start.1 = (bf16[16,1024]{1,0:T(8,128)(2,1)S(1)}, bf16[16,1024]{1,0:T(8,128)(2,1)S(1)}, u32[]{:S(2)}, u32[]{:S(2)}) collective-permute-start(bf16[16,1024]{1,0:T(8,128)(2,1)S(1)} %get-tuple-element.60), channel_id=1, source_target_pairs={{0,3},{1,2},{2,1},{3,0},{4,7},{5,6},{6,5},{7,4},{8,11},{9,10},{10,... | collective-permute-start | bytes 98312 | tf_op jit(solution)/shard_map/ppermute | solution.py:537
  10.2 4.3 %collective-permute-start = (bf16[32,1024]{1,0:T(8,128)(2,1)S(1)}, bf16[32,1024]{1,0:T(8,128)(2,1)S(1)}, u32[]{:S(2)}, u32[]{:S(2)}) collective-permute-start(bf16[32,1024]{1,0:T(8,128)(2,1)S(1)} %get-tuple-element.59.refs_0_), channel_id=1, source_target_pairs={{0,1},{1,0},{2,3},{3,2},{4,6},{5,7},{6,4},{7,5},{8,9},{9,8},{10,11... | collective-permute-start | bytes 196616 | tf_op jit(solution)/shard_map/ppermute | solution.py:546
  12.0 2.5 %collective-permute-start.6 = (bf16[16,4224]{1,0:T(8,128)(2,1)S(1)}, bf16[16,4224]{1,0:T(8,128)(2,1)S(1)}, u32[]{:S(2)}, u32[]{:S(2)}) collective-permute-start(bf16[16,4224]{1,0:T(8,128)(2,1)S(1)} %get-tuple-element.61.refs_0_), channel_id=1, source_target_pairs={{0,4},{4,0},{8,12},{12,8},{16,20},{20,16},{24,28},{28,24},{1,5},{5... | collective-permute-start | bytes 405512 | tf_op jit(solution)/shard_map/ppermute | solution.py:537
  12.6 2.0 %collective-permute-start.9 = (bf16[16,4224]{1,0:T(8,128)(2,1)S(1)}, bf16[16,4224]{1,0:T(8,128)(2,1)S(1)}, u32[]{:S(2)}, u32[]{:S(2)}) collective-permute-start(bf16[16,4224]{1,0:T(8,128)(2,1)S(1)} %collective-permute-done.3.refs_6_), channel_id=1, source_target_pairs={{0,4},{4,0},{8,12},{12,8},{16,20},{20,16},{24,28},{28,24},{1,5},{5... | collective-permute-start | bytes 405512 | tf_op jit(solution)/shard_map/ppermute | solution.py:537
  12.6 2.0 %collective-permute-start.8 = (bf16[16,4224]{1,0:T(8,128)(2,1)S(1)}, bf16[16,4224]{1,0:T(8,128)(2,1)S(1)}, u32[]{:S(2)}, u32[]{:S(2)}) collective-permute-start(bf16[16,4224]{1,0:T(8,128)(2,1)S(1)} %collective-permute-done.4.refs_4_), channel_id=1, source_target_pairs={{0,4},{4,0},{8,12},{12,8},{16,20},{20,16},{24,28},{28,24},{1,5},{5... | collective-permute-start | bytes 405512 | tf_op jit(solution)/shard_map/ppermute | solution.py:537
  13.1 1.5 %collective-permute-start.7 = (bf16[16,4224]{1,0:T(8,128)(2,1)S(1)}, bf16[16,4224]{1,0:T(8,128)(2,1)S(1)}, u32[]{:S(2)}, u32[]{:S(2)}) collective-permute-start(bf16[16,4224]{1,0:T(8,128)(2,1)S(1)} %collective-permute-done.5.refs_2_), channel_id=1, source_target_pairs={{0,4},{4,0},{8,12},{12,8},{16,20},{20,16},{24,28},{28,24},{1,5},{5... | collective-permute-start | bytes 405512 | tf_op jit(solution)/shard_map/ppermute | solution.py:537
  14.5 1.6 %collective-permute-start.2 = (bf16[48,1024]{1,0:T(8,128)(2,1)S(1)}, bf16[48,1024]{1,0:T(8,128)(2,1)S(1)}, u32[]{:S(2)}, u32[]{:S(2)}) collective-permute-start(bf16[48,1024]{1,0:T(8,128)(2,1)S(1)} %shard_map.121.refs_1_), channel_id=1, source_target_pairs={{0,4},{4,0},{8,12},{12,8},{16,20},{20,16},{24,28},{28,24},{1,5},{5... | collective-permute-start | bytes 294920 | tf_op jit(solution)/shard_map/ppermute | solution.py:537
  14.6 1.5 %copy-start.1 = (bf16[1,128,4096]{2,1,0:T(8,128)(2,1)S(1)}, bf16[1,128,4096]{2,1,0:T(8,128)(2,1)}, u32[]{:S(2)}) copy-start(bf16[1,128,4096]{2,1,0:T(8,128)(2,1)} %param.12) | copy-start | bytes 3145732
  14.6 1.5 %copy-start.2 = (bf16[1,16,4096]{2,1,0:T(8,128)(2,1)S(1)}, bf16[1,16,4096]{2,1,0:T(8,128)(2,1)}, u32[]{:S(2)}) copy-start(bf16[1,16,4096]{2,1,0:T(8,128)(2,1)} %param.9) | copy-start | bytes 393220
  14.6 1.5 %copy-start.3 = (bf16[1,16,4096]{2,1,0:T(8,128)(2,1)S(1)}, bf16[1,16,4096]{2,1,0:T(8,128)(2,1)}, u32[]{:S(2)}) copy-start(bf16[1,16,4096]{2,1,0:T(8,128)(2,1)} %param.11) | copy-start | bytes 393220
  17.0 4.7 %collective-permute-start.12 = (f32[32,128]{1,0:T(8,128)S(1)}, f32[32,128]{1,0:T(8,128)S(1)}, u32[]{:S(2)}, u32[]{:S(2)}) collective-permute-start(f32[32,128]{1,0:T(8,128)S(1)} %get-tuple-element.84.refs_0_), channel_id=1, source_target_pairs={{0,24},{4,28},{8,16},{12,20},{16,8},{20,12},{24,0},{28,4},{1,25},{... | collective-permute-start | bytes 49160 | tf_op jit(solution)/shard_map/ppermute | solution.py:537
  19.5 3.7 %collective-permute-start.11 = (f32[32,128]{1,0:T(8,128)S(1)}, f32[32,128]{1,0:T(8,128)S(1)}, u32[]{:S(2)}, u32[]{:S(2)}) collective-permute-start(f32[32,128]{1,0:T(8,128)S(1)} %get-tuple-element.84.refs_0_), channel_id=1, source_target_pairs={{0,16},{4,20},{8,24},{12,28},{16,0},{20,4},{24,8},{28,12},{1,17},{... | collective-permute-start | bytes 49160 | tf_op jit(solution)/shard_map/ppermute | solution.py:537
  20.0 3.7 %collective-permute-start.10 = (f32[32,128]{1,0:T(8,128)S(1)}, f32[32,128]{1,0:T(8,128)S(1)}, u32[]{:S(2)}, u32[]{:S(2)}) collective-permute-start(f32[32,128]{1,0:T(8,128)S(1)} %get-tuple-element.84.refs_0_), channel_id=1, source_target_pairs={{0,8},{4,12},{8,0},{12,4},{16,24},{20,28},{24,16},{28,20},{1,9},{5... | collective-permute-start | bytes 49160 | tf_op jit(solution)/shard_map/ppermute | solution.py:537
  23.7 8.4 %collective-permute-start.14 = (bf16[16,4096]{1,0:T(8,128)(2,1)S(1)}, bf16[16,4096]{1,0:T(8,128)(2,1)S(1)}, u32[]{:S(2)}, u32[]{:S(2)}) collective-permute-start(bf16[16,4096]{1,0:T(8,128)(2,1)S(1)} %get-tuple-element.95), channel_id=1, source_target_pairs={{0,8},{4,12},{8,0},{12,4},{16,24},{20,28},{24,16},{28,20},{1,9},{5... | collective-permute-start | bytes 393224 | tf_op jit(solution)/shard_map/ppermute | solution.py:537
  24.3 3.0 %collective-permute-start.13 = (f32[128,128]{1,0:T(8,128)S(1)}, f32[128,128]{1,0:T(8,128)S(1)}, u32[]{:S(2)}, u32[]{:S(2)}) collective-permute-start(f32[128,128]{1,0:T(8,128)S(1)} %shard_map.126.near_ref), channel_id=1, source_target_pairs={{0,4},{4,0},{8,12},{12,8},{16,20},{20,16},{24,28},{28,24},{1,5},{5... | collective-permute-start | bytes 196616 | tf_op jit(solution)/shard_map/ppermute | solution.py:537
  24.3 14.0 %collective-permute-start.18 = (bf16[16,4096]{1,0:T(8,128)(2,1)S(1)}, bf16[16,4096]{1,0:T(8,128)(2,1)S(1)}, u32[]{:S(2)}, u32[]{:S(2)}) collective-permute-start(bf16[16,4096]{1,0:T(8,128)(2,1)S(1)} %get-tuple-element.102), channel_id=1, source_target_pairs={{0,16},{4,20},{8,24},{12,28},{16,0},{20,4},{24,8},{28,12},{1,17},{... | collective-permute-start | bytes 393224 | tf_op jit(solution)/shard_map/ppermute | solution.py:537
  25.9 12.5 %collective-permute-start.19 = (bf16[16,4096]{1,0:T(8,128)(2,1)S(1)}, bf16[16,4096]{1,0:T(8,128)(2,1)S(1)}, u32[]{:S(2)}, u32[]{:S(2)}) collective-permute-start(bf16[16,4096]{1,0:T(8,128)(2,1)S(1)} %get-tuple-element.103), channel_id=1, source_target_pairs={{0,24},{4,28},{8,16},{12,20},{16,8},{20,12},{24,0},{28,4},{1,25},{... | collective-permute-start | bytes 393224 | tf_op jit(solution)/shard_map/ppermute | solution.py:537
  27.3 5.5 %copy-start = (bf16[1,128,4096]{2,1,0:T(8,128)(2,1)S(1)}, bf16[1,128,4096]{2,1,0:T(8,128)(2,1)}, u32[]{:S(2)}) copy-start(bf16[1,128,4096]{2,1,0:T(8,128)(2,1)} %param.10) | copy-start | bytes 3145732
  28.3 6.6 %collective-permute-start.15 = (bf16[32,1024]{1,0:T(8,128)(2,1)S(1)}, bf16[32,1024]{1,0:T(8,128)(2,1)S(1)}, u32[]{:S(2)}, u32[]{:S(2)}) collective-permute-start(bf16[32,1024]{1,0:T(8,128)(2,1)S(1)} %get-tuple-element.98), channel_id=1, source_target_pairs={{0,1},{1,0},{2,3},{3,2},{4,5},{5,4},{6,7},{7,6},{8,9},{9,8},{10,11... | collective-permute-start | bytes 196616 | tf_op jit(solution)/shard_map/ppermute | solution.py:537
  29.9 7.3 %collective-permute-start.16 = (bf16[32,1024]{1,0:T(8,128)(2,1)S(1)}, bf16[32,1024]{1,0:T(8,128)(2,1)S(1)}, u32[]{:S(2)}, u32[]{:S(2)}) collective-permute-start(bf16[32,1024]{1,0:T(8,128)(2,1)S(1)} %get-tuple-element.99), channel_id=1, source_target_pairs={{0,2},{1,3},{2,0},{3,1},{4,6},{5,7},{6,4},{7,5},{8,10},{9,11},{10,... | collective-permute-start | bytes 196616 | tf_op jit(solution)/shard_map/ppermute | solution.py:537
  32.1 6.2 %collective-permute-start.17 = (bf16[32,1024]{1,0:T(8,128)(2,1)S(1)}, bf16[32,1024]{1,0:T(8,128)(2,1)S(1)}, u32[]{:S(2)}, u32[]{:S(2)}) collective-permute-start(bf16[32,1024]{1,0:T(8,128)(2,1)S(1)} %get-tuple-element.100), channel_id=1, source_target_pairs={{0,3},{1,2},{2,1},{3,0},{4,7},{5,6},{6,5},{7,4},{8,11},{9,10},{10,... | collective-permute-start | bytes 196616 | tf_op jit(solution)/shard_map/ppermute | solution.py:537
  38.4 5.4 %collective-permute-start.21 = (bf16[32,4096]{1,0:T(8,128)(2,1)S(1)}, bf16[32,4096]{1,0:T(8,128)(2,1)S(1)}, u32[]{:S(2)}, u32[]{:S(2)}) collective-permute-start(bf16[32,4096]{1,0:T(8,128)(2,1)S(1)} %shard_map.131), channel_id=1, source_target_pairs={{0,4},{4,0},{8,12},{12,8},{16,20},{20,16},{24,28},{28,24},{1,5},{5... | collective-permute-start | bytes 786440 | tf_op jit(solution)/shard_map/ppermute | solution.py:537
  38.4 1.7 %collective-permute-start.20 = (f32[32,1024]{1,0:T(8,128)S(1)}, f32[32,1024]{1,0:T(8,128)S(1)}, u32[]{:S(2)}, u32[]{:S(2)}) collective-permute-start(f32[32,1024]{1,0:T(8,128)S(1)} %shard_map.129.left_ref), channel_id=1, source_target_pairs={{0,4},{4,0},{8,12},{12,8},{16,20},{20,16},{24,28},{28,24},{1,5},{5... | collective-permute-start | bytes 393224 | tf_op jit(solution)/shard_map/ppermute | solution.py:537
  40.2 5.3 %collective-permute-start.24 = (bf16[32,1024]{1,0:T(8,128)(2,1)S(1)}, bf16[32,1024]{1,0:T(8,128)(2,1)S(1)}, u32[]{:S(2)}, u32[]{:S(2)}) collective-permute-start(bf16[32,1024]{1,0:T(8,128)(2,1)S(1)} %shard_map.130.refs_0_), channel_id=1, source_target_pairs={{0,24},{4,28},{8,16},{12,20},{16,8},{20,12},{24,0},{28,4},{1,25},{... | collective-permute-start | bytes 196616 | tf_op jit(solution)/shard_map/ppermute | solution.py:537
  42.0 4.7 %collective-permute-start.23 = (bf16[32,1024]{1,0:T(8,128)(2,1)S(1)}, bf16[32,1024]{1,0:T(8,128)(2,1)S(1)}, u32[]{:S(2)}, u32[]{:S(2)}) collective-permute-start(bf16[32,1024]{1,0:T(8,128)(2,1)S(1)} %shard_map.130.refs_0_), channel_id=1, source_target_pairs={{0,16},{4,20},{8,24},{12,28},{16,0},{20,4},{24,8},{28,12},{1,17},{... | collective-permute-start | bytes 196616 | tf_op jit(solution)/shard_map/ppermute | solution.py:537
  42.5 4.3 %collective-permute-start.22 = (bf16[32,1024]{1,0:T(8,128)(2,1)S(1)}, bf16[32,1024]{1,0:T(8,128)(2,1)S(1)}, u32[]{:S(2)}, u32[]{:S(2)}) collective-permute-start(bf16[32,1024]{1,0:T(8,128)(2,1)S(1)} %shard_map.130.refs_0_), channel_id=1, source_target_pairs={{0,8},{4,12},{8,0},{12,4},{16,24},{20,28},{24,16},{28,20},{1,9},{5... | collective-permute-start | bytes 196616 | tf_op jit(solution)/shard_map/ppermute | solution.py:537
where the time goes:
time: 47.7 us; the launch traced here: 47.4 us
  starting transfers between devices  25 us (52%)
  Pallas kernels  10.9 us (23%)
  waiting for transfers between devices  10.7 us (22%)
  between operations  0.84 us (2%)
    ppermute x24, starting transfers between devices, exchange(): return lax.ppermute(values, axis, [(i, i ^ k) for i in range(size)])  25 us
    pallas_call x14, Pallas kernels, run(): pl.pallas_call(body, out_shape=out_shape, in_specs=[hbm if in_hbm else vm...  10.9 us
    ppermute x24, waiting for transfers between devices, exchange(): return lax.ppermute(values, axis, [(i, i ^ k) for i in range(size)])  9.38 us
    ppermute x1, waiting for transfers between devices, core_step(): return lax.ppermute(values, ('dp', 'fsdp'), pairs)  1.36 us
  transfers between devices with their start and end apart: 25, of which 11 were waited for; matrix products, arithmetic and copies ran while one was open for 0% of the time, Pallas kernels for 18%

commit v1 on v0

--- a/solution.py
+++ b/solution.py
@@ -250,25 +250,45 @@
     message_ref[HEAD_ROWS:, slots + q_dev :] = unused
 
 
+def near_norm_kernel(width, *refs):
+    out_ref = refs[-1]
+    rows = refs[0].shape[0]
+    chunk = min(width, 1024)
+    for i, ref in enumerate(refs[:-1]):
+        here = slice(i * rows, (i + 1) * rows)
+        inverse = inverse_length(ref, width)
+        for at in range(0, width, chunk):
+            part = ref[:, at : at + chunk].astype(F32)
+            out_ref[here, at : at + chunk] = (part * inverse).astype(BF16)
+        out_ref[here, width:] = ref[:, width:]
+
+
 def score_kernel(group, *refs):
-    blocks = refs[:group]
-    embed_ref, side_ref, positive_ref = refs[group : group + 3]
-    query_ref, weight_ref, dots_ref, onehot_ref, head_ref, coded_ref = refs[group + 3 :]
+    near_ref, *blocks = refs[: group // 2 + 1]
+    embed_ref, side_ref, positive_ref = refs[-9:-6]
+    query_ref, weight_ref, dots_ref, onehot_ref, head_ref, coded_ref = refs[-6:]
     rows, width = embed_ref.shape
     queries = query_ref.shape[0]
     q_dev = queries // group
-    negatives = (blocks[0].shape[1] - width) // 2
+    negatives = (near_ref.shape[1] - width) // 2
     slots = group * CAP
     me = lax.axis_index("dp")
     chunk = min(width, 1024)
     for k in range(group):
         start = pl.multiple_of((me ^ k) * q_dev, q_dev)
-        inverse = inverse_length(blocks[k], width)
+        block = blocks[k // 2]
+        coded_ref[pl.ds(start, q_dev), :] = (
+            near_ref[k // 2 * q_dev : (k // 2 + 1) * q_dev, width:] if k % 2 == 0
+            else block[:, width:]
+        ).astype(F32)
+        if k % 2 == 0:
+            near = near_ref[k // 2 * q_dev : (k // 2 + 1) * q_dev, :width]
+            query_ref[pl.ds(start, q_dev), :] = near
+            continue
+        inverse = inverse_length(block, width)
         for at in range(0, width, chunk):
-            part = blocks[k][:, at : at + chunk].astype(F32)
+            part = block[:, at : at + chunk].astype(F32)
             query_ref[pl.ds(start, q_dev), at : at + chunk] = (part * inverse).astype(BF16)
-        coded = blocks[k][:, width:].astype(F32)
-        coded_ref[pl.ds(start, q_dev), :] = coded
     dots = dot_nt(embed_ref[...], query_ref[...])
     dots_ref[...] = dots
     scores = dots / SOFTMAX_HEAT
@@ -611,9 +631,16 @@
     for k in range(2, group, 2):
         blocks[k], embed = lax.optimization_barrier((blocks[k], embed))
         blocks[k ^ 1] = exchange(blocks[k], "dp", 1)
+    near_queries = run(
+        functools.partial(near_norm_kernel, width),
+        (shape_of((group // 2 * q_dev, packed.shape[1]), BF16),),
+        tuple(blocks[k] for k in range(0, group, 2)),
+        queries * width,
+    )[0]
     if shards == 4:
         half_block = exchange(half, "fsdp", 3)
         whole_block = core_step(adapter, 1, 2)
+        half_block, near_queries = lax.optimization_barrier((half_block, near_queries))
         adapter_near = run(
             join_kernel,
             (shape_of((3 * rank, part), BF16),),
@@ -633,7 +660,8 @@
             shape_of((HEAD_ROWS, queries), F32),
         ),
         (
-            *[blocks[k] for k in range(group)],
+            near_queries,
+            *[blocks[k] for k in range(1, group, 2)],
             embed,
             side,
             positive_row,

time: 47.7 us -> 47.5 us (level)
    pallas_call x14 -> x15, Pallas kernels: 10.9 us -> 11 us  [run(): pl.pallas_call(body, out_shape=out_shape, in_specs=[hbm if in_hbm else vm...]
where the time goes in v1:
time: 47.5 us; the launch traced here: 47.3 us
  starting transfers between devices  25 us (53%)
  Pallas kernels  11 us (23%)
  waiting for transfers between devices  10.5 us (22%)
  between operations  0.84 us (2%)
    ppermute x24, starting transfers between devices, exchange(): return lax.ppermute(values, axis, [(i, i ^ k) for i in range(size)])  25 us
    pallas_call x15, Pallas kernels, run(): pl.pallas_call(body, out_shape=out_shape, in_specs=[hbm if in_hbm else vm...  11 us
    ppermute x24, waiting for transfers between devices, exchange(): return lax.ppermute(values, axis, [(i, i ^ k) for i in range(size)])  9.39 us
    ppermute x1, waiting for transfers between devices, core_step(): return lax.ppermute(values, ('dp', 'fsdp'), pairs)  1.09 us
  transfers between devices with their start and end apart: 25, of which 11 were waited for; matrix products, arithmetic and copies ran while one was open for 0% of the time, Pallas kernels for 18%

profile of v1, /device:TPU:0, one launch (start us, length us, event | category | flops | bytes accessed | tf_op | source)
XLA Modules:
  0.0 47.3 jit_solution(6896039838349287025)
XLA Ops:
  0.6 1.0 %shard_map.120 = (bf16[16,4224]{1,0:T(8,128)(2,1)S(1)}, bf16[32,1024]{1,0:T(8,128)(2,1)S(1)}, bf16[16,1024]{1,0:T(8,128)(2,1)S(1)}, s32[1,128]{1,0:T(1,128)S(1)}) custom-call(bf16[16,4096]{1,0:T(8,128)(2,1)} %bitcast.11, s32[16,64]{1,0:T(8,128)} %bitcast.18, bf16[16,1024]{1,0:T(8,128)(2,1)} %down_ref.1, bf16[16,1024]{1,0:T(8,128)(2,1)} %up_ref.1, ...), custom_call_target="tpu_custom_call" | custom-call | flops 1 | bytes 434752 | tf_op jit(solution)/shard_map/pallas_call | solution.py:64
  1.6 3.0 %collective-permute-start.2 = (bf16[16,4224]{1,0:T(8,128)(2,1)S(1)}, bf16[16,4224]{1,0:T(8,128)(2,1)S(1)}, u32[]{:S(2)}, u32[]{:S(2)}) collective-permute-start(bf16[16,4224]{1,0:T(8,128)(2,1)S(1)} %get-tuple-element.63.refs_0_), channel_id=1, source_target_pairs={{0,8},{4,12},{8,0},{12,4},{16,24},{20,28},{24,16},{28,20},{1,9},{5... | collective-permute-start | bytes 405512 | tf_op jit(solution)/shard_map/ppermute | solution.py:557
  4.6 1.5 %collective-permute-start.3 = (bf16[16,4224]{1,0:T(8,128)(2,1)S(1)}, bf16[16,4224]{1,0:T(8,128)(2,1)S(1)}, u32[]{:S(2)}, u32[]{:S(2)}) collective-permute-start(bf16[16,4224]{1,0:T(8,128)(2,1)S(1)} %get-tuple-element.63.refs_0_), channel_id=1, source_target_pairs={{0,16},{4,20},{8,24},{12,28},{16,0},{20,4},{24,8},{28,12},{1,17},{... | collective-permute-start | bytes 405512 | tf_op jit(solution)/shard_map/ppermute | solution.py:557
  6.2 4.1 %collective-permute-start.1 = (bf16[16,1024]{1,0:T(8,128)(2,1)S(1)}, bf16[16,1024]{1,0:T(8,128)(2,1)S(1)}, u32[]{:S(2)}, u32[]{:S(2)}) collective-permute-start(bf16[16,1024]{1,0:T(8,128)(2,1)S(1)} %get-tuple-element.62), channel_id=1, source_target_pairs={{0,3},{1,2},{2,1},{3,0},{4,7},{5,6},{6,5},{7,4},{8,11},{9,10},{10,... | collective-permute-start | bytes 98312 | tf_op jit(solution)/shard_map/ppermute | solution.py:557
  10.2 1.8 %shard_map.121 = (bf16[128,4096]{1,0:T(8,128)(2,1)S(1)}, f32[128,128]{1,0:T(8,128)S(1)}, f32[8,128]{1,0:T(8,128)S(1)}) custom-call(bf16[128,4096]{1,0:T(8,128)(2,1)} %bitcast.7, s32[1,1024]{1,0:T(1,128)} %home_ref.1), custom_call_target="tpu_custom_call" | custom-call | flops 1048576 | bytes 2170880 | tf_op jit(solution)/shard_map/pallas_call | solution.py:64
  13.4 1.1 %collective-permute-done.first_ref = bf16[32,1024]{1,0:T(8,128)(2,1)S(1)} collective-permute-done((bf16[32,1024]{1,0:T(8,128)(2,1)S(1)}, bf16[32,1024]{1,0:T(8,128)(2,1)S(1)}, u32[]{:S(2)}, u32[]{:S(2)}) %collective-permute-start) | collective-permute-done | bytes 65568 | tf_op jit(solution)/shard_map/ppermute | solution.py:566
  14.6 1.3 %shard_map.124 = (bf16[128,4096]{1,0:T(8,128)(2,1)S(1)}, f32[128,128]{1,0:T(8,128)S(1)}, f32[128,128]{1,0:T(8,128)S(1)}, f32[64,128]{1,0:T(8,128)S(1)}, f32[16,128]{1,0:T(8,128)S(1)}) custom-call(bf16[64,4224]{1,0:T(8,128)(2,1)S(1)} %shard_map.122.refs_0_, bf16[16,4224]{1,0:T(8,128)(2,1)S(1)} %collective-permute-done.6.refs_1_, ...), custom_call_target="tpu_custom_call" | custom-call | flops 134217728 | bytes 3416576 | tf_op jit(solution)/shard_map/pallas_call | solution.py:64
  16.0 0.9 %shard_map.125 = (bf16[32,4096]{1,0:T(8,128)(2,1)S(1)}, f32[16,128]{1,0:T(8,128)S(1)}, f32[32,128]{1,0:T(8,128)S(1)}, f32[8,128]{1,0:T(8,128)S(1)}, f32[16,128]{1,0:T(8,128)S(1)}) custom-call(bf16[32,1024]{1,0:T(8,128)(2,1)S(1)} %get-tuple-element.61.refs_0_, bf16[48,1024]{1,0:T(8,128)(2,1)S(1)} %shard_map.123.refs_1_, ...), custom_call_target="tpu_custom_call" | custom-call | flops 16777216 | bytes 2965504 | tf_op jit(solution)/shard_map/pallas_call | solution.py:64
  16.8 2.5 %collective-permute-start.12 = (f32[32,128]{1,0:T(8,128)S(1)}, f32[32,128]{1,0:T(8,128)S(1)}, u32[]{:S(2)}, u32[]{:S(2)}) collective-permute-start(f32[32,128]{1,0:T(8,128)S(1)} %get-tuple-element.88.refs_0_), channel_id=1, source_target_pairs={{0,24},{4,28},{8,16},{12,20},{16,8},{20,12},{24,0},{28,4},{1,25},{... | collective-permute-start | bytes 49160 | tf_op jit(solution)/shard_map/ppermute | solution.py:557
  19.3 0.5 %collective-permute-start.11 = (f32[32,128]{1,0:T(8,128)S(1)}, f32[32,128]{1,0:T(8,128)S(1)}, u32[]{:S(2)}, u32[]{:S(2)}) collective-permute-start(f32[32,128]{1,0:T(8,128)S(1)} %get-tuple-element.88.refs_0_), channel_id=1, source_target_pairs={{0,16},{4,20},{8,24},{12,28},{16,0},{20,4},{24,8},{28,12},{1,17},{... | collective-permute-start | bytes 49160 | tf_op jit(solution)/shard_map/ppermute | solution.py:557
  19.8 0.5 %collective-permute-start.10 = (f32[32,128]{1,0:T(8,128)S(1)}, f32[32,128]{1,0:T(8,128)S(1)}, u32[]{:S(2)}, u32[]{:S(2)}) collective-permute-start(f32[32,128]{1,0:T(8,128)S(1)} %get-tuple-element.88.refs_0_), channel_id=1, source_target_pairs={{0,8},{4,12},{8,0},{12,4},{16,24},{20,28},{24,16},{28,20},{1,9},{5... | collective-permute-start | bytes 49160 | tf_op jit(solution)/shard_map/ppermute | solution.py:557
  20.4 0.5 %shard_map.126 = (f32[16,128]{1,0:T(8,128)S(1)}, f32[32,128]{1,0:T(8,128)S(1)}, f32[32,128]{1,0:T(8,128)S(1)}, bf16[16,4096]{1,0:T(8,128)(2,1)S(1)}, bf16[16,409...) custom-call(bf16[128,4096]{1,0:T(8,128)(2,1)S(1)} %get-tuple-element.71.refs_5_.refs_6_.refs_0_.refs_4_, ...), custom_call_target="tpu_custom_call" | custom-call | flops 67108864 | bytes 3039744 | tf_op jit(solution)/shard_map/pallas_call | solution.py:64
  20.9 0.6 %collective-permute-done.12.refs_3_ = f32[32,128]{1,0:T(8,128)S(1)} collective-permute-done((f32[32,128]{1,0:T(8,128)S(1)}, f32[32,128]{1,0:T(8,128)S(1)}, u32[]{:S(2)}, u32[]{:S(2)}) %collective-permute-start.12) | collective-permute-done | bytes 16416 | tf_op jit(solution)/shard_map/ppermute | solution.py:557
  21.5 1.5 %collective-permute-done.11.refs_2_ = f32[32,128]{1,0:T(8,128)S(1)} collective-permute-done((f32[32,128]{1,0:T(8,128)S(1)}, f32[32,128]{1,0:T(8,128)S(1)}, u32[]{:S(2)}, u32[]{:S(2)}) %collective-permute-start.11) | collective-permute-done | bytes 16416 | tf_op jit(solution)/shard_map/ppermute | solution.py:557
  23.1 0.5 %collective-permute-done.10.refs_1_ = f32[32,128]{1,0:T(8,128)S(1)} collective-permute-done((f32[32,128]{1,0:T(8,128)S(1)}, f32[32,128]{1,0:T(8,128)S(1)}, u32[]{:S(2)}, u32[]{:S(2)}) %collective-permute-start.10) | collective-permute-done | bytes 16416 | tf_op jit(solution)/shard_map/ppermute | solution.py:557
  23.6 0.5 %collective-permute-start.14 = (bf16[16,4096]{1,0:T(8,128)(2,1)S(1)}, bf16[16,4096]{1,0:T(8,128)(2,1)S(1)}, u32[]{:S(2)}, u32[]{:S(2)}) collective-permute-start(bf16[16,4096]{1,0:T(8,128)(2,1)S(1)} %get-tuple-element.99), channel_id=1, source_target_pairs={{0,8},{4,12},{8,0},{12,4},{16,24},{20,28},{24,16},{28,20},{1,9},{5... | collective-permute-start | bytes 393224 | tf_op jit(solution)/shard_map/ppermute | solution.py:557
  24.1 1.6 %collective-permute-start.18 = (bf16[16,4096]{1,0:T(8,128)(2,1)S(1)}, bf16[16,4096]{1,0:T(8,128)(2,1)S(1)}, u32[]{:S(2)}, u32[]{:S(2)}) collective-permute-start(bf16[16,4096]{1,0:T(8,128)(2,1)S(1)} %get-tuple-element.106), channel_id=1, source_target_pairs={{0,16},{4,20},{8,24},{12,28},{16,0},{20,4},{24,8},{28,12},{1,17},{... | collective-permute-start | bytes 393224 | tf_op jit(solution)/shard_map/ppermute | solution.py:557
  25.7 1.4 %collective-permute-start.19 = (bf16[16,4096]{1,0:T(8,128)(2,1)S(1)}, bf16[16,4096]{1,0:T(8,128)(2,1)S(1)}, u32[]{:S(2)}, u32[]{:S(2)}) collective-permute-start(bf16[16,4096]{1,0:T(8,128)(2,1)S(1)} %get-tuple-element.107), channel_id=1, source_target_pairs={{0,24},{4,28},{8,16},{12,20},{16,8},{20,12},{24,0},{28,4},{1,25},{... | collective-permute-start | bytes 393224 | tf_op jit(solution)/shard_map/ppermute | solution.py:557
  27.2 1.0 %shard_map.128 = (f32[128,128]{1,0:T(8,128)S(1)}, f32[32,1024]{1,0:T(8,128)S(1)}, bf16[32,1024]{1,0:T(8,128)(2,1)S(1)}, bf16[32,1024]{1,0:T(8,128)(2,1)S(1)}, bf16[32,1024]{1,0:T(8,128)(2,1)S(1)}) custom-call(f32[128,128]{1,0:T(8,128)S(1)} %shard_map.127.near_ref, f32[128,128]{1,0:T(8,128)S(1)} %collective-permute-done.13.far_ref, ...), custom_call_target="tpu_custom_call" | custom-call | flops 67108864 | bytes 3998208 | tf_op jit(solution)/shard_map/pallas_call | solution.py:64
  28.2 1.6 %collective-permute-start.15 = (bf16[32,1024]{1,0:T(8,128)(2,1)S(1)}, bf16[32,1024]{1,0:T(8,128)(2,1)S(1)}, u32[]{:S(2)}, u32[]{:S(2)}) collective-permute-start(bf16[32,1024]{1,0:T(8,128)(2,1)S(1)} %get-tuple-element.102), channel_id=1, source_target_pairs={{0,1},{1,0},{2,3},{3,2},{4,5},{5,4},{6,7},{7,6},{8,9},{9,8},{10,11... | collective-permute-start | bytes 196616 | tf_op jit(solution)/shard_map/ppermute | solution.py:557
  29.8 2.2 %collective-permute-start.16 = (bf16[32,1024]{1,0:T(8,128)(2,1)S(1)}, bf16[32,1024]{1,0:T(8,128)(2,1)S(1)}, u32[]{:S(2)}, u32[]{:S(2)}) collective-permute-start(bf16[32,1024]{1,0:T(8,128)(2,1)S(1)} %get-tuple-element.103), channel_id=1, source_target_pairs={{0,2},{1,3},{2,0},{3,1},{4,6},{5,7},{6,4},{7,5},{8,10},{9,11},{10,... | collective-permute-start | bytes 196616 | tf_op jit(solution)/shard_map/ppermute | solution.py:557
  32.0 0.7 %collective-permute-start.17 = (bf16[32,1024]{1,0:T(8,128)(2,1)S(1)}, bf16[32,1024]{1,0:T(8,128)(2,1)S(1)}, u32[]{:S(2)}, u32[]{:S(2)}) collective-permute-start(bf16[32,1024]{1,0:T(8,128)(2,1)S(1)} %get-tuple-element.104), channel_id=1, source_target_pairs={{0,3},{1,2},{2,1},{3,0},{4,7},{5,6},{6,5},{7,4},{8,11},{9,10},{10,... | collective-permute-start | bytes 196616 | tf_op jit(solution)/shard_map/ppermute | solution.py:557
  32.7 2.2 %shard_map.129 = bf16[128,4096]{1,0:T(8,128)(2,1)} custom-call(f32[128,128]{1,0:T(8,128)S(1)} %get-tuple-element.100.final_ref.refs_4_, bf16[128,4096]{1,0:T(8,128)(2,1)S(1)} %get-tuple-element.79.refs_2_.refs_3_.query_ref, bf16[128,4096]{1,0:T(8,128)(2,1)S(1)} %bitcast.8, f32[128,128]{1,0:T(8,128)S(1)} %get-tuple-element.74.refs_6_.side_ref), custom_call_target="tpu_custom_call" | custom-call | flops 268435456 | bytes 3276800 | tf_op jit(solution)/shard_map/pallas_call | solution.py:64
  34.8 2.3 %collective-permute-done.16.refs_2_ = bf16[32,1024]{1,0:T(8,128)(2,1)S(1)} collective-permute-done((bf16[32,1024]{1,0:T(8,128)(2,1)S(1)}, bf16[32,1024]{1,0:T(8,128)(2,1)S(1)}, u32[]{:S(2)}, u32[]{:S(2)}) %collective-permute-start.16) | collective-permute-done | bytes 65568 | tf_op jit(solution)/shard_map/ppermute | solution.py:557
  37.1 1.0 %collective-permute-done.17.refs_3_ = bf16[32,1024]{1,0:T(8,128)(2,1)S(1)} collective-permute-done((bf16[32,1024]{1,0:T(8,128)(2,1)S(1)}, bf16[32,1024]{1,0:T(8,128)(2,1)S(1)}, u32[]{:S(2)}, u32[]{:S(2)}) %collective-permute-start.17) | collective-permute-done | bytes 65568 | tf_op jit(solution)/shard_map/ppermute | solution.py:557
  38.8 1.2 %collective-permute-done.20.right_ref = f32[32,1024]{1,0:T(8,128)S(1)} collective-permute-done((f32[32,1024]{1,0:T(8,128)S(1)}, f32[32,1024]{1,0:T(8,128)S(1)}, u32[]{:S(2)}, u32[]{:S(2)}) %collective-permute-start.20) | collective-permute-done | bytes 131104 | tf_op jit(solution)/shard_map/ppermute | solution.py:557
  40.0 1.8 %collective-permute-start.24 = (bf16[32,1024]{1,0:T(8,128)(2,1)S(1)}, bf16[32,1024]{1,0:T(8,128)(2,1)S(1)}, u32[]{:S(2)}, u32[]{:S(2)}) collective-permute-start(bf16[32,1024]{1,0:T(8,128)(2,1)S(1)} %shard_map.131.refs_0_), channel_id=1, source_target_pairs={{0,24},{4,28},{8,16},{12,20},{16,8},{20,12},{24,0},{28,4},{1,25},{... | collective-permute-start | bytes 196616 | tf_op jit(solution)/shard_map/ppermute | solution.py:557
  41.8 0.5 %collective-permute-start.23 = (bf16[32,1024]{1,0:T(8,128)(2,1)S(1)}, bf16[32,1024]{1,0:T(8,128)(2,1)S(1)}, u32[]{:S(2)}, u32[]{:S(2)}) collective-permute-start(bf16[32,1024]{1,0:T(8,128)(2,1)S(1)} %shard_map.131.refs_0_), channel_id=1, source_target_pairs={{0,16},{4,20},{8,24},{12,28},{16,0},{20,4},{24,8},{28,12},{1,17},{... | collective-permute-start | bytes 196616 | tf_op jit(solution)/shard_map/ppermute | solution.py:557
  42.4 1.2 %collective-permute-start.22 = (bf16[32,1024]{1,0:T(8,128)(2,1)S(1)}, bf16[32,1024]{1,0:T(8,128)(2,1)S(1)}, u32[]{:S(2)}, u32[]{:S(2)}) collective-permute-start(bf16[32,1024]{1,0:T(8,128)(2,1)S(1)} %shard_map.131.refs_0_), channel_id=1, source_target_pairs={{0,8},{4,12},{8,0},{12,4},{16,24},{20,28},{24,16},{28,20},{1,9},{5... | collective-permute-start | bytes 196616 | tf_op jit(solution)/shard_map/ppermute | solution.py:557
  43.6 1.3 %shard_map.133 = bf16[16,4096]{1,0:T(8,128)(2,1)} custom-call(f32[128,128]{1,0:T(8,128)S(1)} %shard_map.127.near_ref, f32[128,128]{1,0:T(8,128)S(1)} %collective-permute-done.13.far_ref, bf16[16,4096]{1,0:T(8,128)(2,1)S(1)} %collective-permute-done.14.refs_1_.refs_0_, bf16[16,4096]{1,0:T(8,128)(2,1)S(1)} %collective-permute-done.18.refs_2_.refs_1_, ...), custom_call_target="tpu_custom_call" | custom-call | flops 50331648 | bytes 2162688 | tf_op jit(solution)/shard_map/pallas_call | solution.py:64
  45.3 1.2 %collective-permute-done.23.refs_2_ = bf16[32,1024]{1,0:T(8,128)(2,1)S(1)} collective-permute-done((bf16[32,1024]{1,0:T(8,128)(2,1)S(1)}, bf16[32,1024]{1,0:T(8,128)(2,1)S(1)}, u32[]{:S(2)}, u32[]{:S(2)}) %collective-permute-start.23) | collective-permute-done | bytes 65568 | tf_op jit(solution)/shard_map/ppermute | solution.py:557
  46.6 0.7 %shard_map.134 = (f32[16,1024]{1,0:T(8,128)}, f32[16,1024]{1,0:T(8,128)}) custom-call(bf16[32,1024]{1,0:T(8,128)(2,1)S(1)} %shard_map.131.refs_0_, bf16[32,1024]{1,0:T(8,128)(2,1)S(1)} %collective-permute-done.22.refs_1_, bf16[32,1024]{1,0:T(8,128)(2,1)S(1)} %collective-permute-done.23.refs_2_, bf16[32,1024]{1,0:T(8,128)(2,1)S(1)} %collective-permute-done.24.refs_3_), custom_call_target="tpu_custom_call" | custom-call | flops 1 | bytes 393216 | tf_op jit(solution)/shard_map/pallas_call | solution.py:64
  (41 shorter events, 2.6 us)
Async XLA Ops:
  1.6 10.4 %collective-permute-start.2 = (bf16[16,4224]{1,0:T(8,128)(2,1)S(1)}, bf16[16,4224]{1,0:T(8,128)(2,1)S(1)}, u32[]{:S(2)}, u32[]{:S(2)}) collective-permute-start(bf16[16,4224]{1,0:T(8,128)(2,1)S(1)} %get-tuple-element.63.refs_0_), channel_id=1, source_target_pairs={{0,8},{4,12},{8,0},{12,4},{16,24},{20,28},{24,16},{28,20},{1,9},{5... | collective-permute-start | bytes 405512 | tf_op jit(solution)/shard_map/ppermute | solution.py:557
  4.6 7.9 %collective-permute-start.3 = (bf16[16,4224]{1,0:T(8,128)(2,1)S(1)}, bf16[16,4224]{1,0:T(8,128)(2,1)S(1)}, u32[]{:S(2)}, u32[]{:S(2)}) collective-permute-start(bf16[16,4224]{1,0:T(8,128)(2,1)S(1)} %get-tuple-element.63.refs_0_), channel_id=1, source_target_pairs={{0,16},{4,20},{8,24},{12,28},{16,0},{20,4},{24,8},{28,12},{1,17},{... | collective-permute-start | bytes 405512 | tf_op jit(solution)/shard_map/ppermute | solution.py:557
  6.1 6.4 %collective-permute-start.4 = (bf16[16,4224]{1,0:T(8,128)(2,1)S(1)}, bf16[16,4224]{1,0:T(8,128)(2,1)S(1)}, u32[]{:S(2)}, u32[]{:S(2)}) collective-permute-start(bf16[16,4224]{1,0:T(8,128)(2,1)S(1)} %get-tuple-element.63.refs_0_), channel_id=1, source_target_pairs={{0,24},{4,28},{8,16},{12,20},{16,8},{20,12},{24,0},{28,4},{1,25},{... | collective-permute-start | bytes 405512 | tf_op jit(solution)/shard_map/ppermute | solution.py:557
  6.2 6.9 %collective-permute-start.1 = (bf16[16,1024]{1,0:T(8,128)(2,1)S(1)}, bf16[16,1024]{1,0:T(8,128)(2,1)S(1)}, u32[]{:S(2)}, u32[]{:S(2)}) collective-permute-start(bf16[16,1024]{1,0:T(8,128)(2,1)S(1)} %get-tuple-element.62), channel_id=1, source_target_pairs={{0,3},{1,2},{2,1},{3,0},{4,7},{5,6},{6,5},{7,4},{8,11},{9,10},{10,... | collective-permute-start | bytes 98312 | tf_op jit(solution)/shard_map/ppermute | solution.py:557
  10.2 4.3 %collective-permute-start = (bf16[32,1024]{1,0:T(8,128)(2,1)S(1)}, bf16[32,1024]{1,0:T(8,128)(2,1)S(1)}, u32[]{:S(2)}, u32[]{:S(2)}) collective-permute-start(bf16[32,1024]{1,0:T(8,128)(2,1)S(1)} %get-tuple-element.61.refs_0_), channel_id=1, source_target_pairs={{0,1},{1,0},{2,3},{3,2},{4,6},{5,7},{6,4},{7,5},{8,9},{9,8},{10,11... | collective-permute-start | bytes 196616 | tf_op jit(solution)/shard_map/ppermute | solution.py:566
  12.0 2.5 %collective-permute-start.6 = (bf16[16,4224]{1,0:T(8,128)(2,1)S(1)}, bf16[16,4224]{1,0:T(8,128)(2,1)S(1)}, u32[]{:S(2)}, u32[]{:S(2)}) collective-permute-start(bf16[16,4224]{1,0:T(8,128)(2,1)S(1)} %get-tuple-element.63.refs_0_), channel_id=1, source_target_pairs={{0,4},{4,0},{8,12},{12,8},{16,20},{20,16},{24,28},{28,24},{1,5},{5... | collective-permute-start | bytes 405512 | tf_op jit(solution)/shard_map/ppermute | solution.py:557
  12.6 2.0 %collective-permute-start.9 = (bf16[16,4224]{1,0:T(8,128)(2,1)S(1)}, bf16[16,4224]{1,0:T(8,128)(2,1)S(1)}, u32[]{:S(2)}, u32[]{:S(2)}) collective-permute-start(bf16[16,4224]{1,0:T(8,128)(2,1)S(1)} %collective-permute-done.4.refs_3_), channel_id=1, source_target_pairs={{0,4},{4,0},{8,12},{12,8},{16,20},{20,16},{24,28},{28,24},{1,5},{5... | collective-permute-start | bytes 405512 | tf_op jit(solution)/shard_map/ppermute | solution.py:557
  12.6 2.0 %collective-permute-start.8 = (bf16[16,4224]{1,0:T(8,128)(2,1)S(1)}, bf16[16,4224]{1,0:T(8,128)(2,1)S(1)}, u32[]{:S(2)}, u32[]{:S(2)}) collective-permute-start(bf16[16,4224]{1,0:T(8,128)(2,1)S(1)} %collective-permute-done.3.refs_2_), channel_id=1, source_target_pairs={{0,4},{4,0},{8,12},{12,8},{16,20},{20,16},{24,28},{28,24},{1,5},{5... | collective-permute-start | bytes 405512 | tf_op jit(solution)/shard_map/ppermute | solution.py:557
  13.1 1.5 %collective-permute-start.7 = (bf16[16,4224]{1,0:T(8,128)(2,1)S(1)}, bf16[16,4224]{1,0:T(8,128)(2,1)S(1)}, u32[]{:S(2)}, u32[]{:S(2)}) collective-permute-start(bf16[16,4224]{1,0:T(8,128)(2,1)S(1)} %collective-permute-done.2.refs_1_), channel_id=1, source_target_pairs={{0,4},{4,0},{8,12},{12,8},{16,20},{20,16},{24,28},{28,24},{1,5},{5... | collective-permute-start | bytes 405512 | tf_op jit(solution)/shard_map/ppermute | solution.py:557
  14.5 1.4 %collective-permute-start.5 = (bf16[48,1024]{1,0:T(8,128)(2,1)S(1)}, bf16[48,1024]{1,0:T(8,128)(2,1)S(1)}, u32[]{:S(2)}, u32[]{:S(2)}) collective-permute-start(bf16[48,1024]{1,0:T(8,128)(2,1)S(1)} %shard_map.123.refs_1_), channel_id=1, source_target_pairs={{0,4},{4,0},{8,12},{12,8},{16,20},{20,16},{24,28},{28,24},{1,5},{5... | collective-permute-start | bytes 294920 | tf_op jit(solution)/shard_map/ppermute | solution.py:557
  14.6 1.3 %copy-start.1 = (bf16[1,128,4096]{2,1,0:T(8,128)(2,1)S(1)}, bf16[1,128,4096]{2,1,0:T(8,128)(2,1)}, u32[]{:S(2)}) copy-start(bf16[1,128,4096]{2,1,0:T(8,128)(2,1)} %param.12) | copy-start | bytes 3145732
  14.6 1.3 %copy-start.2 = (bf16[1,16,4096]{2,1,0:T(8,128)(2,1)S(1)}, bf16[1,16,4096]{2,1,0:T(8,128)(2,1)}, u32[]{:S(2)}) copy-start(bf16[1,16,4096]{2,1,0:T(8,128)(2,1)} %param.9) | copy-start | bytes 393220
  14.6 1.3 %copy-start.3 = (bf16[1,16,4096]{2,1,0:T(8,128)(2,1)S(1)}, bf16[1,16,4096]{2,1,0:T(8,128)(2,1)}, u32[]{:S(2)}) copy-start(bf16[1,16,4096]{2,1,0:T(8,128)(2,1)} %param.11) | copy-start | bytes 393220
  16.8 4.7 %collective-permute-start.12 = (f32[32,128]{1,0:T(8,128)S(1)}, f32[32,128]{1,0:T(8,128)S(1)}, u32[]{:S(2)}, u32[]{:S(2)}) collective-permute-start(f32[32,128]{1,0:T(8,128)S(1)} %get-tuple-element.88.refs_0_), channel_id=1, source_target_pairs={{0,24},{4,28},{8,16},{12,20},{16,8},{20,12},{24,0},{28,4},{1,25},{... | collective-permute-start | bytes 49160 | tf_op jit(solution)/shard_map/ppermute | solution.py:557
  19.3 3.7 %collective-permute-start.11 = (f32[32,128]{1,0:T(8,128)S(1)}, f32[32,128]{1,0:T(8,128)S(1)}, u32[]{:S(2)}, u32[]{:S(2)}) collective-permute-start(f32[32,128]{1,0:T(8,128)S(1)} %get-tuple-element.88.refs_0_), channel_id=1, source_target_pairs={{0,16},{4,20},{8,24},{12,28},{16,0},{20,4},{24,8},{28,12},{1,17},{... | collective-permute-start | bytes 49160 | tf_op jit(solution)/shard_map/ppermute | solution.py:557
  19.8 3.7 %collective-permute-start.10 = (f32[32,128]{1,0:T(8,128)S(1)}, f32[32,128]{1,0:T(8,128)S(1)}, u32[]{:S(2)}, u32[]{:S(2)}) collective-permute-start(f32[32,128]{1,0:T(8,128)S(1)} %get-tuple-element.88.refs_0_), channel_id=1, source_target_pairs={{0,8},{4,12},{8,0},{12,4},{16,24},{20,28},{24,16},{28,20},{1,9},{5... | collective-permute-start | bytes 49160 | tf_op jit(solution)/shard_map/ppermute | solution.py:557
  23.6 8.4 %collective-permute-start.14 = (bf16[16,4096]{1,0:T(8,128)(2,1)S(1)}, bf16[16,4096]{1,0:T(8,128)(2,1)S(1)}, u32[]{:S(2)}, u32[]{:S(2)}) collective-permute-start(bf16[16,4096]{1,0:T(8,128)(2,1)S(1)} %get-tuple-element.99), channel_id=1, source_target_pairs={{0,8},{4,12},{8,0},{12,4},{16,24},{20,28},{24,16},{28,20},{1,9},{5... | collective-permute-start | bytes 393224 | tf_op jit(solution)/shard_map/ppermute | solution.py:557
  24.1 3.0 %collective-permute-start.13 = (f32[128,128]{1,0:T(8,128)S(1)}, f32[128,128]{1,0:T(8,128)S(1)}, u32[]{:S(2)}, u32[]{:S(2)}) collective-permute-start(f32[128,128]{1,0:T(8,128)S(1)} %shard_map.127.near_ref), channel_id=1, source_target_pairs={{0,4},{4,0},{8,12},{12,8},{16,20},{20,16},{24,28},{28,24},{1,5},{5... | collective-permute-start | bytes 196616 | tf_op jit(solution)/shard_map/ppermute | solution.py:557
  24.1 14.0 %collective-permute-start.18 = (bf16[16,4096]{1,0:T(8,128)(2,1)S(1)}, bf16[16,4096]{1,0:T(8,128)(2,1)S(1)}, u32[]{:S(2)}, u32[]{:S(2)}) collective-permute-start(bf16[16,4096]{1,0:T(8,128)(2,1)S(1)} %get-tuple-element.106), channel_id=1, source_target_pairs={{0,16},{4,20},{8,24},{12,28},{16,0},{20,4},{24,8},{28,12},{1,17},{... | collective-permute-start | bytes 393224 | tf_op jit(solution)/shard_map/ppermute | solution.py:557
  25.7 12.5 %collective-permute-start.19 = (bf16[16,4096]{1,0:T(8,128)(2,1)S(1)}, bf16[16,4096]{1,0:T(8,128)(2,1)S(1)}, u32[]{:S(2)}, u32[]{:S(2)}) collective-permute-start(bf16[16,4096]{1,0:T(8,128)(2,1)S(1)} %get-tuple-element.107), channel_id=1, source_target_pairs={{0,24},{4,28},{8,16},{12,20},{16,8},{20,12},{24,0},{28,4},{1,25},{... | collective-permute-start | bytes 393224 | tf_op jit(solution)/shard_map/ppermute | solution.py:557
  27.2 5.5 %copy-start = (bf16[1,128,4096]{2,1,0:T(8,128)(2,1)S(1)}, bf16[1,128,4096]{2,1,0:T(8,128)(2,1)}, u32[]{:S(2)}) copy-start(bf16[1,128,4096]{2,1,0:T(8,128)(2,1)} %param.10) | copy-start | bytes 3145732
  28.2 6.6 %collective-permute-start.15 = (bf16[32,1024]{1,0:T(8,128)(2,1)S(1)}, bf16[32,1024]{1,0:T(8,128)(2,1)S(1)}, u32[]{:S(2)}, u32[]{:S(2)}) collective-permute-start(bf16[32,1024]{1,0:T(8,128)(2,1)S(1)} %get-tuple-element.102), channel_id=1, source_target_pairs={{0,1},{1,0},{2,3},{3,2},{4,5},{5,4},{6,7},{7,6},{8,9},{9,8},{10,11... | collective-permute-start | bytes 196616 | tf_op jit(solution)/shard_map/ppermute | solution.py:557
  29.8 7.3 %collective-permute-start.16 = (bf16[32,1024]{1,0:T(8,128)(2,1)S(1)}, bf16[32,1024]{1,0:T(8,128)(2,1)S(1)}, u32[]{:S(2)}, u32[]{:S(2)}) collective-permute-start(bf16[32,1024]{1,0:T(8,128)(2,1)S(1)} %get-tuple-element.103), channel_id=1, source_target_pairs={{0,2},{1,3},{2,0},{3,1},{4,6},{5,7},{6,4},{7,5},{8,10},{9,11},{10,... | collective-permute-start | bytes 196616 | tf_op jit(solution)/shard_map/ppermute | solution.py:557
  32.0 6.2 %collective-permute-start.17 = (bf16[32,1024]{1,0:T(8,128)(2,1)S(1)}, bf16[32,1024]{1,0:T(8,128)(2,1)S(1)}, u32[]{:S(2)}, u32[]{:S(2)}) collective-permute-start(bf16[32,1024]{1,0:T(8,128)(2,1)S(1)} %get-tuple-element.104), channel_id=1, source_target_pairs={{0,3},{1,2},{2,1},{3,0},{4,7},{5,6},{6,5},{7,4},{8,11},{9,10},{10,... | collective-permute-start | bytes 196616 | tf_op jit(solution)/shard_map/ppermute | solution.py:557
  38.2 5.4 %collective-permute-start.21 = (bf16[32,4096]{1,0:T(8,128)(2,1)S(1)}, bf16[32,4096]{1,0:T(8,128)(2,1)S(1)}, u32[]{:S(2)}, u32[]{:S(2)}) collective-permute-start(bf16[32,4096]{1,0:T(8,128)(2,1)S(1)} %shard_map.132), channel_id=1, source_target_pairs={{0,4},{4,0},{8,12},{12,8},{16,20},{20,16},{24,28},{28,24},{1,5},{5... | collective-permute-start | bytes 786440 | tf_op jit(solution)/shard_map/ppermute | solution.py:557
  38.3 1.7 %collective-permute-start.20 = (f32[32,1024]{1,0:T(8,128)S(1)}, f32[32,1024]{1,0:T(8,128)S(1)}, u32[]{:S(2)}, u32[]{:S(2)}) collective-permute-start(f32[32,1024]{1,0:T(8,128)S(1)} %shard_map.130.left_ref), channel_id=1, source_target_pairs={{0,4},{4,0},{8,12},{12,8},{16,20},{20,16},{24,28},{28,24},{1,5},{5... | collective-permute-start | bytes 393224 | tf_op jit(solution)/shard_map/ppermute | solution.py:557
  40.0 5.3 %collective-permute-start.24 = (bf16[32,1024]{1,0:T(8,128)(2,1)S(1)}, bf16[32,1024]{1,0:T(8,128)(2,1)S(1)}, u32[]{:S(2)}, u32[]{:S(2)}) collective-permute-start(bf16[32,1024]{1,0:T(8,128)(2,1)S(1)} %shard_map.131.refs_0_), channel_id=1, source_target_pairs={{0,24},{4,28},{8,16},{12,20},{16,8},{20,12},{24,0},{28,4},{1,25},{... | collective-permute-start | bytes 196616 | tf_op jit(solution)/shard_map/ppermute | solution.py:557
  41.8 4.7 %collective-permute-start.23 = (bf16[32,1024]{1,0:T(8,128)(2,1)S(1)}, bf16[32,1024]{1,0:T(8,128)(2,1)S(1)}, u32[]{:S(2)}, u32[]{:S(2)}) collective-permute-start(bf16[32,1024]{1,0:T(8,128)(2,1)S(1)} %shard_map.131.refs_0_), channel_id=1, source_target_pairs={{0,16},{4,20},{8,24},{12,28},{16,0},{20,4},{24,8},{28,12},{1,17},{... | collective-permute-start | bytes 196616 | tf_op jit(solution)/shard_map/ppermute | solution.py:557
  42.4 4.3 %collective-permute-start.22 = (bf16[32,1024]{1,0:T(8,128)(2,1)S(1)}, bf16[32,1024]{1,0:T(8,128)(2,1)S(1)}, u32[]{:S(2)}, u32[]{:S(2)}) collective-permute-start(bf16[32,1024]{1,0:T(8,128)(2,1)S(1)} %shard_map.131.refs_0_), channel_id=1, source_target_pairs={{0,8},{4,12},{8,0},{12,4},{16,24},{20,28},{24,16},{28,20},{1,9},{5... | collective-permute-start | bytes 196616 | tf_op jit(solution)/shard_map/ppermute | solution.py:557

commit v2 on v1

--- a/solution.py
+++ b/solution.py
@@ -462,7 +462,7 @@
     pick = (iota((q_dev, queries), 1) == iota((q_dev, queries), 0) + me * q_dev).astype(BF16)
     back_query = dot_nt(back_query.astype(BF16), pick).astype(BF16)
 
-    chunk = min(width, 512)
+    chunk = min(width, 2048)
     for at in range(0, width, chunk):
         cols = slice(at, at + chunk)
         both = dot_nn(query_parts, query_ref[:, cols]) + dot_nn(passage_parts, embed_ref[:, cols])

time: 47.5 us -> 47.4 us (level)
  no operation moved by 1% of the time
where the time goes in v2:
time: 47.4 us; the launch traced here: 47.2 us
  starting transfers between devices  25 us (53%)
  Pallas kernels  10.9 us (23%)
  waiting for transfers between devices  10.5 us (22%)
  between operations  0.84 us (2%)
    ppermute x24, starting transfers between devices, exchange(): return lax.ppermute(values, axis, [(i, i ^ k) for i in range(size)])  25 us
    pallas_call x15, Pallas kernels, run(): pl.pallas_call(body, out_shape=out_shape, in_specs=[hbm if in_hbm else vm...  10.9 us
    ppermute x24, waiting for transfers between devices, exchange(): return lax.ppermute(values, axis, [(i, i ^ k) for i in range(size)])  9.39 us
    ppermute x1, waiting for transfers between devices, core_step(): return lax.ppermute(values, ('dp', 'fsdp'), pairs)  1.09 us
  transfers between devices with their start and end apart: 25, of which 11 were waited for; matrix products, arithmetic and copies ran while one was open for 0% of the time, Pallas kernels for 18%

profile of v2, /device:TPU:0, one launch (start us, length us, event | category | flops | bytes accessed | tf_op | source)
XLA Modules:
  0.0 47.2 jit_solution(12551037075550189999)
XLA Ops:
  0.6 1.0 %shard_map.120 = (bf16[16,4224]{1,0:T(8,128)(2,1)S(1)}, bf16[32,1024]{1,0:T(8,128)(2,1)S(1)}, bf16[16,1024]{1,0:T(8,128)(2,1)S(1)}, s32[1,128]{1,0:T(1,128)S(1)}) custom-call(bf16[16,4096]{1,0:T(8,128)(2,1)} %bitcast.11, s32[16,64]{1,0:T(8,128)} %bitcast.18, bf16[16,1024]{1,0:T(8,128)(2,1)} %down_ref.1, bf16[16,1024]{1,0:T(8,128)(2,1)} %up_ref.1, ...), custom_call_target="tpu_custom_call" | custom-call | flops 1 | bytes 434752 | tf_op jit(solution)/shard_map/pallas_call | solution.py:64
  1.6 3.0 %collective-permute-start.2 = (bf16[16,4224]{1,0:T(8,128)(2,1)S(1)}, bf16[16,4224]{1,0:T(8,128)(2,1)S(1)}, u32[]{:S(2)}, u32[]{:S(2)}) collective-permute-start(bf16[16,4224]{1,0:T(8,128)(2,1)S(1)} %get-tuple-element.63.refs_0_), channel_id=1, source_target_pairs={{0,8},{4,12},{8,0},{12,4},{16,24},{20,28},{24,16},{28,20},{1,9},{5... | collective-permute-start | bytes 405512 | tf_op jit(solution)/shard_map/ppermute | solution.py:557
  4.6 1.5 %collective-permute-start.3 = (bf16[16,4224]{1,0:T(8,128)(2,1)S(1)}, bf16[16,4224]{1,0:T(8,128)(2,1)S(1)}, u32[]{:S(2)}, u32[]{:S(2)}) collective-permute-start(bf16[16,4224]{1,0:T(8,128)(2,1)S(1)} %get-tuple-element.63.refs_0_), channel_id=1, source_target_pairs={{0,16},{4,20},{8,24},{12,28},{16,0},{20,4},{24,8},{28,12},{1,17},{... | collective-permute-start | bytes 405512 | tf_op jit(solution)/shard_map/ppermute | solution.py:557
  6.2 4.1 %collective-permute-start.1 = (bf16[16,1024]{1,0:T(8,128)(2,1)S(1)}, bf16[16,1024]{1,0:T(8,128)(2,1)S(1)}, u32[]{:S(2)}, u32[]{:S(2)}) collective-permute-start(bf16[16,1024]{1,0:T(8,128)(2,1)S(1)} %get-tuple-element.62), channel_id=1, source_target_pairs={{0,3},{1,2},{2,1},{3,0},{4,7},{5,6},{6,5},{7,4},{8,11},{9,10},{10,... | collective-permute-start | bytes 98312 | tf_op jit(solution)/shard_map/ppermute | solution.py:557
  10.2 1.8 %shard_map.121 = (bf16[128,4096]{1,0:T(8,128)(2,1)S(1)}, f32[128,128]{1,0:T(8,128)S(1)}, f32[8,128]{1,0:T(8,128)S(1)}) custom-call(bf16[128,4096]{1,0:T(8,128)(2,1)} %bitcast.7, s32[1,1024]{1,0:T(1,128)} %home_ref.1), custom_call_target="tpu_custom_call" | custom-call | flops 1048576 | bytes 2170880 | tf_op jit(solution)/shard_map/pallas_call | solution.py:64
  13.4 1.1 %collective-permute-done.first_ref = bf16[32,1024]{1,0:T(8,128)(2,1)S(1)} collective-permute-done((bf16[32,1024]{1,0:T(8,128)(2,1)S(1)}, bf16[32,1024]{1,0:T(8,128)(2,1)S(1)}, u32[]{:S(2)}, u32[]{:S(2)}) %collective-permute-start) | collective-permute-done | bytes 65568 | tf_op jit(solution)/shard_map/ppermute | solution.py:566
  14.6 1.3 %shard_map.124 = (bf16[128,4096]{1,0:T(8,128)(2,1)S(1)}, f32[128,128]{1,0:T(8,128)S(1)}, f32[128,128]{1,0:T(8,128)S(1)}, f32[64,128]{1,0:T(8,128)S(1)}, f32[16,128]{1,0:T(8,128)S(1)}) custom-call(bf16[64,4224]{1,0:T(8,128)(2,1)S(1)} %shard_map.122.refs_0_, bf16[16,4224]{1,0:T(8,128)(2,1)S(1)} %collective-permute-done.6.refs_1_, ...), custom_call_target="tpu_custom_call" | custom-call | flops 134217728 | bytes 3416576 | tf_op jit(solution)/shard_map/pallas_call | solution.py:64
  16.0 0.9 %shard_map.125 = (bf16[32,4096]{1,0:T(8,128)(2,1)S(1)}, f32[16,128]{1,0:T(8,128)S(1)}, f32[32,128]{1,0:T(8,128)S(1)}, f32[8,128]{1,0:T(8,128)S(1)}, f32[16,128]{1,0:T(8,128)S(1)}) custom-call(bf16[32,1024]{1,0:T(8,128)(2,1)S(1)} %get-tuple-element.61.refs_0_, bf16[48,1024]{1,0:T(8,128)(2,1)S(1)} %shard_map.123.refs_1_, ...), custom_call_target="tpu_custom_call" | custom-call | flops 16777216 | bytes 2965504 | tf_op jit(solution)/shard_map/pallas_call | solution.py:64
  16.8 2.5 %collective-permute-start.12 = (f32[32,128]{1,0:T(8,128)S(1)}, f32[32,128]{1,0:T(8,128)S(1)}, u32[]{:S(2)}, u32[]{:S(2)}) collective-permute-start(f32[32,128]{1,0:T(8,128)S(1)} %get-tuple-element.88.refs_0_), channel_id=1, source_target_pairs={{0,24},{4,28},{8,16},{12,20},{16,8},{20,12},{24,0},{28,4},{1,25},{... | collective-permute-start | bytes 49160 | tf_op jit(solution)/shard_map/ppermute | solution.py:557
  19.3 0.5 %collective-permute-start.11 = (f32[32,128]{1,0:T(8,128)S(1)}, f32[32,128]{1,0:T(8,128)S(1)}, u32[]{:S(2)}, u32[]{:S(2)}) collective-permute-start(f32[32,128]{1,0:T(8,128)S(1)} %get-tuple-element.88.refs_0_), channel_id=1, source_target_pairs={{0,16},{4,20},{8,24},{12,28},{16,0},{20,4},{24,8},{28,12},{1,17},{... | collective-permute-start | bytes 49160 | tf_op jit(solution)/shard_map/ppermute | solution.py:557
  19.8 0.5 %collective-permute-start.10 = (f32[32,128]{1,0:T(8,128)S(1)}, f32[32,128]{1,0:T(8,128)S(1)}, u32[]{:S(2)}, u32[]{:S(2)}) collective-permute-start(f32[32,128]{1,0:T(8,128)S(1)} %get-tuple-element.88.refs_0_), channel_id=1, source_target_pairs={{0,8},{4,12},{8,0},{12,4},{16,24},{20,28},{24,16},{28,20},{1,9},{5... | collective-permute-start | bytes 49160 | tf_op jit(solution)/shard_map/ppermute | solution.py:557
  20.4 0.5 %shard_map.126 = (f32[16,128]{1,0:T(8,128)S(1)}, f32[32,128]{1,0:T(8,128)S(1)}, f32[32,128]{1,0:T(8,128)S(1)}, bf16[16,4096]{1,0:T(8,128)(2,1)S(1)}, bf16[16,409...) custom-call(bf16[128,4096]{1,0:T(8,128)(2,1)S(1)} %get-tuple-element.71.refs_5_.refs_6_.refs_0_.refs_4_, ...), custom_call_target="tpu_custom_call" | custom-call | flops 67108864 | bytes 3039744 | tf_op jit(solution)/shard_map/pallas_call | solution.py:64
  20.9 0.6 %collective-permute-done.12.refs_3_ = f32[32,128]{1,0:T(8,128)S(1)} collective-permute-done((f32[32,128]{1,0:T(8,128)S(1)}, f32[32,128]{1,0:T(8,128)S(1)}, u32[]{:S(2)}, u32[]{:S(2)}) %collective-permute-start.12) | collective-permute-done | bytes 16416 | tf_op jit(solution)/shard_map/ppermute | solution.py:557
  21.5 1.5 %collective-permute-done.11.refs_2_ = f32[32,128]{1,0:T(8,128)S(1)} collective-permute-done((f32[32,128]{1,0:T(8,128)S(1)}, f32[32,128]{1,0:T(8,128)S(1)}, u32[]{:S(2)}, u32[]{:S(2)}) %collective-permute-start.11) | collective-permute-done | bytes 16416 | tf_op jit(solution)/shard_map/ppermute | solution.py:557
  23.1 0.5 %collective-permute-done.10.refs_1_ = f32[32,128]{1,0:T(8,128)S(1)} collective-permute-done((f32[32,128]{1,0:T(8,128)S(1)}, f32[32,128]{1,0:T(8,128)S(1)}, u32[]{:S(2)}, u32[]{:S(2)}) %collective-permute-start.10) | collective-permute-done | bytes 16416 | tf_op jit(solution)/shard_map/ppermute | solution.py:557
  23.6 0.5 %collective-permute-start.14 = (bf16[16,4096]{1,0:T(8,128)(2,1)S(1)}, bf16[16,4096]{1,0:T(8,128)(2,1)S(1)}, u32[]{:S(2)}, u32[]{:S(2)}) collective-permute-start(bf16[16,4096]{1,0:T(8,128)(2,1)S(1)} %get-tuple-element.99), channel_id=1, source_target_pairs={{0,8},{4,12},{8,0},{12,4},{16,24},{20,28},{24,16},{28,20},{1,9},{5... | collective-permute-start | bytes 393224 | tf_op jit(solution)/shard_map/ppermute | solution.py:557
  24.1 1.6 %collective-permute-start.18 = (bf16[16,4096]{1,0:T(8,128)(2,1)S(1)}, bf16[16,4096]{1,0:T(8,128)(2,1)S(1)}, u32[]{:S(2)}, u32[]{:S(2)}) collective-permute-start(bf16[16,4096]{1,0:T(8,128)(2,1)S(1)} %get-tuple-element.106), channel_id=1, source_target_pairs={{0,16},{4,20},{8,24},{12,28},{16,0},{20,4},{24,8},{28,12},{1,17},{... | collective-permute-start | bytes 393224 | tf_op jit(solution)/shard_map/ppermute | solution.py:557
  25.7 1.4 %collective-permute-start.19 = (bf16[16,4096]{1,0:T(8,128)(2,1)S(1)}, bf16[16,4096]{1,0:T(8,128)(2,1)S(1)}, u32[]{:S(2)}, u32[]{:S(2)}) collective-permute-start(bf16[16,4096]{1,0:T(8,128)(2,1)S(1)} %get-tuple-element.107), channel_id=1, source_target_pairs={{0,24},{4,28},{8,16},{12,20},{16,8},{20,12},{24,0},{28,4},{1,25},{... | collective-permute-start | bytes 393224 | tf_op jit(solution)/shard_map/ppermute | solution.py:557
  27.2 0.9 %shard_map.128 = (f32[128,128]{1,0:T(8,128)S(1)}, f32[32,1024]{1,0:T(8,128)S(1)}, bf16[32,1024]{1,0:T(8,128)(2,1)S(1)}, bf16[32,1024]{1,0:T(8,128)(2,1)S(1)}, bf16[32,1024]{1,0:T(8,128)(2,1)S(1)}) custom-call(f32[128,128]{1,0:T(8,128)S(1)} %shard_map.127.near_ref, f32[128,128]{1,0:T(8,128)S(1)} %collective-permute-done.13.far_ref, ...), custom_call_target="tpu_custom_call" | custom-call | flops 67108864 | bytes 3998208 | tf_op jit(solution)/shard_map/pallas_call | solution.py:64
  28.1 1.6 %collective-permute-start.15 = (bf16[32,1024]{1,0:T(8,128)(2,1)S(1)}, bf16[32,1024]{1,0:T(8,128)(2,1)S(1)}, u32[]{:S(2)}, u32[]{:S(2)}) collective-permute-start(bf16[32,1024]{1,0:T(8,128)(2,1)S(1)} %get-tuple-element.102), channel_id=1, source_target_pairs={{0,1},{1,0},{2,3},{3,2},{4,5},{5,4},{6,7},{7,6},{8,9},{9,8},{10,11... | collective-permute-start | bytes 196616 | tf_op jit(solution)/shard_map/ppermute | solution.py:557
  29.7 2.2 %collective-permute-start.16 = (bf16[32,1024]{1,0:T(8,128)(2,1)S(1)}, bf16[32,1024]{1,0:T(8,128)(2,1)S(1)}, u32[]{:S(2)}, u32[]{:S(2)}) collective-permute-start(bf16[32,1024]{1,0:T(8,128)(2,1)S(1)} %get-tuple-element.103), channel_id=1, source_target_pairs={{0,2},{1,3},{2,0},{3,1},{4,6},{5,7},{6,4},{7,5},{8,10},{9,11},{10,... | collective-permute-start | bytes 196616 | tf_op jit(solution)/shard_map/ppermute | solution.py:557
  31.9 0.7 %collective-permute-start.17 = (bf16[32,1024]{1,0:T(8,128)(2,1)S(1)}, bf16[32,1024]{1,0:T(8,128)(2,1)S(1)}, u32[]{:S(2)}, u32[]{:S(2)}) collective-permute-start(bf16[32,1024]{1,0:T(8,128)(2,1)S(1)} %get-tuple-element.104), channel_id=1, source_target_pairs={{0,3},{1,2},{2,1},{3,0},{4,7},{5,6},{6,5},{7,4},{8,11},{9,10},{10,... | collective-permute-start | bytes 196616 | tf_op jit(solution)/shard_map/ppermute | solution.py:557
  32.6 2.2 %shard_map.129 = bf16[128,4096]{1,0:T(8,128)(2,1)} custom-call(f32[128,128]{1,0:T(8,128)S(1)} %get-tuple-element.100.final_ref.refs_4_, bf16[128,4096]{1,0:T(8,128)(2,1)S(1)} %get-tuple-element.79.refs_2_.refs_3_.query_ref, bf16[128,4096]{1,0:T(8,128)(2,1)S(1)} %bitcast.8, f32[128,128]{1,0:T(8,128)S(1)} %get-tuple-element.74.refs_6_.side_ref), custom_call_target="tpu_custom_call" | custom-call | flops 268435456 | bytes 3276800 | tf_op jit(solution)/shard_map/pallas_call | solution.py:64
  34.7 2.3 %collective-permute-done.16.refs_2_ = bf16[32,1024]{1,0:T(8,128)(2,1)S(1)} collective-permute-done((bf16[32,1024]{1,0:T(8,128)(2,1)S(1)}, bf16[32,1024]{1,0:T(8,128)(2,1)S(1)}, u32[]{:S(2)}, u32[]{:S(2)}) %collective-permute-start.16) | collective-permute-done | bytes 65568 | tf_op jit(solution)/shard_map/ppermute | solution.py:557
  37.0 1.0 %collective-permute-done.17.refs_3_ = bf16[32,1024]{1,0:T(8,128)(2,1)S(1)} collective-permute-done((bf16[32,1024]{1,0:T(8,128)(2,1)S(1)}, bf16[32,1024]{1,0:T(8,128)(2,1)S(1)}, u32[]{:S(2)}, u32[]{:S(2)}) %collective-permute-start.17) | collective-permute-done | bytes 65568 | tf_op jit(solution)/shard_map/ppermute | solution.py:557
  38.7 1.2 %collective-permute-done.20.right_ref = f32[32,1024]{1,0:T(8,128)S(1)} collective-permute-done((f32[32,1024]{1,0:T(8,128)S(1)}, f32[32,1024]{1,0:T(8,128)S(1)}, u32[]{:S(2)}, u32[]{:S(2)}) %collective-permute-start.20) | collective-permute-done | bytes 131104 | tf_op jit(solution)/shard_map/ppermute | solution.py:557
  39.9 1.8 %collective-permute-start.24 = (bf16[32,1024]{1,0:T(8,128)(2,1)S(1)}, bf16[32,1024]{1,0:T(8,128)(2,1)S(1)}, u32[]{:S(2)}, u32[]{:S(2)}) collective-permute-start(bf16[32,1024]{1,0:T(8,128)(2,1)S(1)} %shard_map.131.refs_0_), channel_id=1, source_target_pairs={{0,24},{4,28},{8,16},{12,20},{16,8},{20,12},{24,0},{28,4},{1,25},{... | collective-permute-start | bytes 196616 | tf_op jit(solution)/shard_map/ppermute | solution.py:557
  41.7 0.5 %collective-permute-start.23 = (bf16[32,1024]{1,0:T(8,128)(2,1)S(1)}, bf16[32,1024]{1,0:T(8,128)(2,1)S(1)}, u32[]{:S(2)}, u32[]{:S(2)}) collective-permute-start(bf16[32,1024]{1,0:T(8,128)(2,1)S(1)} %shard_map.131.refs_0_), channel_id=1, source_target_pairs={{0,16},{4,20},{8,24},{12,28},{16,0},{20,4},{24,8},{28,12},{1,17},{... | collective-permute-start | bytes 196616 | tf_op jit(solution)/shard_map/ppermute | solution.py:557
  42.3 1.2 %collective-permute-start.22 = (bf16[32,1024]{1,0:T(8,128)(2,1)S(1)}, bf16[32,1024]{1,0:T(8,128)(2,1)S(1)}, u32[]{:S(2)}, u32[]{:S(2)}) collective-permute-start(bf16[32,1024]{1,0:T(8,128)(2,1)S(1)} %shard_map.131.refs_0_), channel_id=1, source_target_pairs={{0,8},{4,12},{8,0},{12,4},{16,24},{20,28},{24,16},{28,20},{1,9},{5... | collective-permute-start | bytes 196616 | tf_op jit(solution)/shard_map/ppermute | solution.py:557
  43.5 1.3 %shard_map.133 = bf16[16,4096]{1,0:T(8,128)(2,1)} custom-call(f32[128,128]{1,0:T(8,128)S(1)} %shard_map.127.near_ref, f32[128,128]{1,0:T(8,128)S(1)} %collective-permute-done.13.far_ref, bf16[16,4096]{1,0:T(8,128)(2,1)S(1)} %collective-permute-done.14.refs_1_.refs_0_, bf16[16,4096]{1,0:T(8,128)(2,1)S(1)} %collective-permute-done.18.refs_2_.refs_1_, ...), custom_call_target="tpu_custom_call" | custom-call | flops 50331648 | bytes 2162688 | tf_op jit(solution)/shard_map/pallas_call | solution.py:64
  45.2 1.2 %collective-permute-done.23.refs_2_ = bf16[32,1024]{1,0:T(8,128)(2,1)S(1)} collective-permute-done((bf16[32,1024]{1,0:T(8,128)(2,1)S(1)}, bf16[32,1024]{1,0:T(8,128)(2,1)S(1)}, u32[]{:S(2)}, u32[]{:S(2)}) %collective-permute-start.23) | collective-permute-done | bytes 65568 | tf_op jit(solution)/shard_map/ppermute | solution.py:557
  46.5 0.7 %shard_map.134 = (f32[16,1024]{1,0:T(8,128)}, f32[16,1024]{1,0:T(8,128)}) custom-call(bf16[32,1024]{1,0:T(8,128)(2,1)S(1)} %shard_map.131.refs_0_, bf16[32,1024]{1,0:T(8,128)(2,1)S(1)} %collective-permute-done.22.refs_1_, bf16[32,1024]{1,0:T(8,128)(2,1)S(1)} %collective-permute-done.23.refs_2_, bf16[32,1024]{1,0:T(8,128)(2,1)S(1)} %collective-permute-done.24.refs_3_), custom_call_target="tpu_custom_call" | custom-call | flops 1 | bytes 393216 | tf_op jit(solution)/shard_map/pallas_call | solution.py:64
  (41 shorter events, 2.6 us)
Async XLA Ops:
  1.6 10.4 %collective-permute-start.2 = (bf16[16,4224]{1,0:T(8,128)(2,1)S(1)}, bf16[16,4224]{1,0:T(8,128)(2,1)S(1)}, u32[]{:S(2)}, u32[]{:S(2)}) collective-permute-start(bf16[16,4224]{1,0:T(8,128)(2,1)S(1)} %get-tuple-element.63.refs_0_), channel_id=1, source_target_pairs={{0,8},{4,12},{8,0},{12,4},{16,24},{20,28},{24,16},{28,20},{1,9},{5... | collective-permute-start | bytes 405512 | tf_op jit(solution)/shard_map/ppermute | solution.py:557
  4.6 7.9 %collective-permute-start.3 = (bf16[16,4224]{1,0:T(8,128)(2,1)S(1)}, bf16[16,4224]{1,0:T(8,128)(2,1)S(1)}, u32[]{:S(2)}, u32[]{:S(2)}) collective-permute-start(bf16[16,4224]{1,0:T(8,128)(2,1)S(1)} %get-tuple-element.63.refs_0_), channel_id=1, source_target_pairs={{0,16},{4,20},{8,24},{12,28},{16,0},{20,4},{24,8},{28,12},{1,17},{... | collective-permute-start | bytes 405512 | tf_op jit(solution)/shard_map/ppermute | solution.py:557
  6.1 6.4 %collective-permute-start.4 = (bf16[16,4224]{1,0:T(8,128)(2,1)S(1)}, bf16[16,4224]{1,0:T(8,128)(2,1)S(1)}, u32[]{:S(2)}, u32[]{:S(2)}) collective-permute-start(bf16[16,4224]{1,0:T(8,128)(2,1)S(1)} %get-tuple-element.63.refs_0_), channel_id=1, source_target_pairs={{0,24},{4,28},{8,16},{12,20},{16,8},{20,12},{24,0},{28,4},{1,25},{... | collective-permute-start | bytes 405512 | tf_op jit(solution)/shard_map/ppermute | solution.py:557
  6.2 6.9 %collective-permute-start.1 = (bf16[16,1024]{1,0:T(8,128)(2,1)S(1)}, bf16[16,1024]{1,0:T(8,128)(2,1)S(1)}, u32[]{:S(2)}, u32[]{:S(2)}) collective-permute-start(bf16[16,1024]{1,0:T(8,128)(2,1)S(1)} %get-tuple-element.62), channel_id=1, source_target_pairs={{0,3},{1,2},{2,1},{3,0},{4,7},{5,6},{6,5},{7,4},{8,11},{9,10},{10,... | collective-permute-start | bytes 98312 | tf_op jit(solution)/shard_map/ppermute | solution.py:557
  10.2 4.3 %collective-permute-start = (bf16[32,1024]{1,0:T(8,128)(2,1)S(1)}, bf16[32,1024]{1,0:T(8,128)(2,1)S(1)}, u32[]{:S(2)}, u32[]{:S(2)}) collective-permute-start(bf16[32,1024]{1,0:T(8,128)(2,1)S(1)} %get-tuple-element.61.refs_0_), channel_id=1, source_target_pairs={{0,1},{1,0},{2,3},{3,2},{4,6},{5,7},{6,4},{7,5},{8,9},{9,8},{10,11... | collective-permute-start | bytes 196616 | tf_op jit(solution)/shard_map/ppermute | solution.py:566
  12.0 2.5 %collective-permute-start.6 = (bf16[16,4224]{1,0:T(8,128)(2,1)S(1)}, bf16[16,4224]{1,0:T(8,128)(2,1)S(1)}, u32[]{:S(2)}, u32[]{:S(2)}) collective-permute-start(bf16[16,4224]{1,0:T(8,128)(2,1)S(1)} %get-tuple-element.63.refs_0_), channel_id=1, source_target_pairs={{0,4},{4,0},{8,12},{12,8},{16,20},{20,16},{24,28},{28,24},{1,5},{5... | collective-permute-start | bytes 405512 | tf_op jit(solution)/shard_map/ppermute | solution.py:557
  12.6 2.0 %collective-permute-start.9 = (bf16[16,4224]{1,0:T(8,128)(2,1)S(1)}, bf16[16,4224]{1,0:T(8,128)(2,1)S(1)}, u32[]{:S(2)}, u32[]{:S(2)}) collective-permute-start(bf16[16,4224]{1,0:T(8,128)(2,1)S(1)} %collective-permute-done.4.refs_3_), channel_id=1, source_target_pairs={{0,4},{4,0},{8,12},{12,8},{16,20},{20,16},{24,28},{28,24},{1,5},{5... | collective-permute-start | bytes 405512 | tf_op jit(solution)/shard_map/ppermute | solution.py:557
  12.6 2.0 %collective-permute-start.8 = (bf16[16,4224]{1,0:T(8,128)(2,1)S(1)}, bf16[16,4224]{1,0:T(8,128)(2,1)S(1)}, u32[]{:S(2)}, u32[]{:S(2)}) collective-permute-start(bf16[16,4224]{1,0:T(8,128)(2,1)S(1)} %collective-permute-done.3.refs_2_), channel_id=1, source_target_pairs={{0,4},{4,0},{8,12},{12,8},{16,20},{20,16},{24,28},{28,24},{1,5},{5... | collective-permute-start | bytes 405512 | tf_op jit(solution)/shard_map/ppermute | solution.py:557
  13.1 1.5 %collective-permute-start.7 = (bf16[16,4224]{1,0:T(8,128)(2,1)S(1)}, bf16[16,4224]{1,0:T(8,128)(2,1)S(1)}, u32[]{:S(2)}, u32[]{:S(2)}) collective-permute-start(bf16[16,4224]{1,0:T(8,128)(2,1)S(1)} %collective-permute-done.2.refs_1_), channel_id=1, source_target_pairs={{0,4},{4,0},{8,12},{12,8},{16,20},{20,16},{24,28},{28,24},{1,5},{5... | collective-permute-start | bytes 405512 | tf_op jit(solution)/shard_map/ppermute | solution.py:557
  14.5 1.4 %collective-permute-start.5 = (bf16[48,1024]{1,0:T(8,128)(2,1)S(1)}, bf16[48,1024]{1,0:T(8,128)(2,1)S(1)}, u32[]{:S(2)}, u32[]{:S(2)}) collective-permute-start(bf16[48,1024]{1,0:T(8,128)(2,1)S(1)} %shard_map.123.refs_1_), channel_id=1, source_target_pairs={{0,4},{4,0},{8,12},{12,8},{16,20},{20,16},{24,28},{28,24},{1,5},{5... | collective-permute-start | bytes 294920 | tf_op jit(solution)/shard_map/ppermute | solution.py:557
  14.6 1.3 %copy-start.1 = (bf16[1,128,4096]{2,1,0:T(8,128)(2,1)S(1)}, bf16[1,128,4096]{2,1,0:T(8,128)(2,1)}, u32[]{:S(2)}) copy-start(bf16[1,128,4096]{2,1,0:T(8,128)(2,1)} %param.12) | copy-start | bytes 3145732
  14.6 1.3 %copy-start.2 = (bf16[1,16,4096]{2,1,0:T(8,128)(2,1)S(1)}, bf16[1,16,4096]{2,1,0:T(8,128)(2,1)}, u32[]{:S(2)}) copy-start(bf16[1,16,4096]{2,1,0:T(8,128)(2,1)} %param.9) | copy-start | bytes 393220
  14.6 1.3 %copy-start.3 = (bf16[1,16,4096]{2,1,0:T(8,128)(2,1)S(1)}, bf16[1,16,4096]{2,1,0:T(8,128)(2,1)}, u32[]{:S(2)}) copy-start(bf16[1,16,4096]{2,1,0:T(8,128)(2,1)} %param.11) | copy-start | bytes 393220
  16.8 4.7 %collective-permute-start.12 = (f32[32,128]{1,0:T(8,128)S(1)}, f32[32,128]{1,0:T(8,128)S(1)}, u32[]{:S(2)}, u32[]{:S(2)}) collective-permute-start(f32[32,128]{1,0:T(8,128)S(1)} %get-tuple-element.88.refs_0_), channel_id=1, source_target_pairs={{0,24},{4,28},{8,16},{12,20},{16,8},{20,12},{24,0},{28,4},{1,25},{... | collective-permute-start | bytes 49160 | tf_op jit(solution)/shard_map/ppermute | solution.py:557
  19.3 3.7 %collective-permute-start.11 = (f32[32,128]{1,0:T(8,128)S(1)}, f32[32,128]{1,0:T(8,128)S(1)}, u32[]{:S(2)}, u32[]{:S(2)}) collective-permute-start(f32[32,128]{1,0:T(8,128)S(1)} %get-tuple-element.88.refs_0_), channel_id=1, source_target_pairs={{0,16},{4,20},{8,24},{12,28},{16,0},{20,4},{24,8},{28,12},{1,17},{... | collective-permute-start | bytes 49160 | tf_op jit(solution)/shard_map/ppermute | solution.py:557
  19.8 3.7 %collective-permute-start.10 = (f32[32,128]{1,0:T(8,128)S(1)}, f32[32,128]{1,0:T(8,128)S(1)}, u32[]{:S(2)}, u32[]{:S(2)}) collective-permute-start(f32[32,128]{1,0:T(8,128)S(1)} %get-tuple-element.88.refs_0_), channel_id=1, source_target_pairs={{0,8},{4,12},{8,0},{12,4},{16,24},{20,28},{24,16},{28,20},{1,9},{5... | collective-permute-start | bytes 49160 | tf_op jit(solution)/shard_map/ppermute | solution.py:557
  23.6 8.3 %collective-permute-start.14 = (bf16[16,4096]{1,0:T(8,128)(2,1)S(1)}, bf16[16,4096]{1,0:T(8,128)(2,1)S(1)}, u32[]{:S(2)}, u32[]{:S(2)}) collective-permute-start(bf16[16,4096]{1,0:T(8,128)(2,1)S(1)} %get-tuple-element.99), channel_id=1, source_target_pairs={{0,8},{4,12},{8,0},{12,4},{16,24},{20,28},{24,16},{28,20},{1,9},{5... | collective-permute-start | bytes 393224 | tf_op jit(solution)/shard_map/ppermute | solution.py:557
  24.1 3.0 %collective-permute-start.13 = (f32[128,128]{1,0:T(8,128)S(1)}, f32[128,128]{1,0:T(8,128)S(1)}, u32[]{:S(2)}, u32[]{:S(2)}) collective-permute-start(f32[128,128]{1,0:T(8,128)S(1)} %shard_map.127.near_ref), channel_id=1, source_target_pairs={{0,4},{4,0},{8,12},{12,8},{16,20},{20,16},{24,28},{28,24},{1,5},{5... | collective-permute-start | bytes 196616 | tf_op jit(solution)/shard_map/ppermute | solution.py:557
  24.1 13.9 %collective-permute-start.18 = (bf16[16,4096]{1,0:T(8,128)(2,1)S(1)}, bf16[16,4096]{1,0:T(8,128)(2,1)S(1)}, u32[]{:S(2)}, u32[]{:S(2)}) collective-permute-start(bf16[16,4096]{1,0:T(8,128)(2,1)S(1)} %get-tuple-element.106), channel_id=1, source_target_pairs={{0,16},{4,20},{8,24},{12,28},{16,0},{20,4},{24,8},{28,12},{1,17},{... | collective-permute-start | bytes 393224 | tf_op jit(solution)/shard_map/ppermute | solution.py:557
  25.7 12.4 %collective-permute-start.19 = (bf16[16,4096]{1,0:T(8,128)(2,1)S(1)}, bf16[16,4096]{1,0:T(8,128)(2,1)S(1)}, u32[]{:S(2)}, u32[]{:S(2)}) collective-permute-start(bf16[16,4096]{1,0:T(8,128)(2,1)S(1)} %get-tuple-element.107), channel_id=1, source_target_pairs={{0,24},{4,28},{8,16},{12,20},{16,8},{20,12},{24,0},{28,4},{1,25},{... | collective-permute-start | bytes 393224 | tf_op jit(solution)/shard_map/ppermute | solution.py:557
  27.2 5.4 %copy-start = (bf16[1,128,4096]{2,1,0:T(8,128)(2,1)S(1)}, bf16[1,128,4096]{2,1,0:T(8,128)(2,1)}, u32[]{:S(2)}) copy-start(bf16[1,128,4096]{2,1,0:T(8,128)(2,1)} %param.10) | copy-start | bytes 3145732
  28.1 6.6 %collective-permute-start.15 = (bf16[32,1024]{1,0:T(8,128)(2,1)S(1)}, bf16[32,1024]{1,0:T(8,128)(2,1)S(1)}, u32[]{:S(2)}, u32[]{:S(2)}) collective-permute-start(bf16[32,1024]{1,0:T(8,128)(2,1)S(1)} %get-tuple-element.102), channel_id=1, source_target_pairs={{0,1},{1,0},{2,3},{3,2},{4,5},{5,4},{6,7},{7,6},{8,9},{9,8},{10,11... | collective-permute-start | bytes 196616 | tf_op jit(solution)/shard_map/ppermute | solution.py:557
  29.7 7.3 %collective-permute-start.16 = (bf16[32,1024]{1,0:T(8,128)(2,1)S(1)}, bf16[32,1024]{1,0:T(8,128)(2,1)S(1)}, u32[]{:S(2)}, u32[]{:S(2)}) collective-permute-start(bf16[32,1024]{1,0:T(8,128)(2,1)S(1)} %get-tuple-element.103), channel_id=1, source_target_pairs={{0,2},{1,3},{2,0},{3,1},{4,6},{5,7},{6,4},{7,5},{8,10},{9,11},{10,... | collective-permute-start | bytes 196616 | tf_op jit(solution)/shard_map/ppermute | solution.py:557
  31.9 6.2 %collective-permute-start.17 = (bf16[32,1024]{1,0:T(8,128)(2,1)S(1)}, bf16[32,1024]{1,0:T(8,128)(2,1)S(1)}, u32[]{:S(2)}, u32[]{:S(2)}) collective-permute-start(bf16[32,1024]{1,0:T(8,128)(2,1)S(1)} %get-tuple-element.104), channel_id=1, source_target_pairs={{0,3},{1,2},{2,1},{3,0},{4,7},{5,6},{6,5},{7,4},{8,11},{9,10},{10,... | collective-permute-start | bytes 196616 | tf_op jit(solution)/shard_map/ppermute | solution.py:557
  38.1 5.4 %collective-permute-start.21 = (bf16[32,4096]{1,0:T(8,128)(2,1)S(1)}, bf16[32,4096]{1,0:T(8,128)(2,1)S(1)}, u32[]{:S(2)}, u32[]{:S(2)}) collective-permute-start(bf16[32,4096]{1,0:T(8,128)(2,1)S(1)} %shard_map.132), channel_id=1, source_target_pairs={{0,4},{4,0},{8,12},{12,8},{16,20},{20,16},{24,28},{28,24},{1,5},{5... | collective-permute-start | bytes 786440 | tf_op jit(solution)/shard_map/ppermute | solution.py:557
  38.2 1.7 %collective-permute-start.20 = (f32[32,1024]{1,0:T(8,128)S(1)}, f32[32,1024]{1,0:T(8,128)S(1)}, u32[]{:S(2)}, u32[]{:S(2)}) collective-permute-start(f32[32,1024]{1,0:T(8,128)S(1)} %shard_map.130.left_ref), channel_id=1, source_target_pairs={{0,4},{4,0},{8,12},{12,8},{16,20},{20,16},{24,28},{28,24},{1,5},{5... | collective-permute-start | bytes 393224 | tf_op jit(solution)/shard_map/ppermute | solution.py:557
  39.9 5.3 %collective-permute-start.24 = (bf16[32,1024]{1,0:T(8,128)(2,1)S(1)}, bf16[32,1024]{1,0:T(8,128)(2,1)S(1)}, u32[]{:S(2)}, u32[]{:S(2)}) collective-permute-start(bf16[32,1024]{1,0:T(8,128)(2,1)S(1)} %shard_map.131.refs_0_), channel_id=1, source_target_pairs={{0,24},{4,28},{8,16},{12,20},{16,8},{20,12},{24,0},{28,4},{1,25},{... | collective-permute-start | bytes 196616 | tf_op jit(solution)/shard_map/ppermute | solution.py:557
  41.7 4.7 %collective-permute-start.23 = (bf16[32,1024]{1,0:T(8,128)(2,1)S(1)}, bf16[32,1024]{1,0:T(8,128)(2,1)S(1)}, u32[]{:S(2)}, u32[]{:S(2)}) collective-permute-start(bf16[32,1024]{1,0:T(8,128)(2,1)S(1)} %shard_map.131.refs_0_), channel_id=1, source_target_pairs={{0,16},{4,20},{8,24},{12,28},{16,0},{20,4},{24,8},{28,12},{1,17},{... | collective-permute-start | bytes 196616 | tf_op jit(solution)/shard_map/ppermute | solution.py:557
  42.3 4.3 %collective-permute-start.22 = (bf16[32,1024]{1,0:T(8,128)(2,1)S(1)}, bf16[32,1024]{1,0:T(8,128)(2,1)S(1)}, u32[]{:S(2)}, u32[]{:S(2)}) collective-permute-start(bf16[32,1024]{1,0:T(8,128)(2,1)S(1)} %shard_map.131.refs_0_), channel_id=1, source_target_pairs={{0,8},{4,12},{8,0},{12,4},{16,24},{20,28},{24,16},{28,20},{1,9},{5... | collective-permute-start | bytes 196616 | tf_op jit(solution)/shard_map/ppermute | solution.py:557
